TPU v7x, 256 devices: a whole 4x4x8 slice. The times are simulated.
256 devices in a mesh: grp: 8 (over z), gz: 32 (over x, y, core).
Axes of the slice: x: 4, y: 4, z: 8, core: 2. Of those that a mesh axis runs over, the one named last changes fastest.
Arguments:
- spectrum: float32 [2, 3, 256, 256, 256], P(None, None, ('grp', 'gz')), may hold values from -16 to 16
- marker_fraction: float32 [8192, 3, 256], P(('grp', 'gz')), may hold values from 0 to 1
- marker_offsets: int32 [8192, 3, 256], P(('grp', 'gz')), may hold values from 0 to 8, as said below
- block_source: int32 [8192, 1], P(('grp', 'gz')), may hold values from 0 to 31; in each aligned block of 32 rows (0 to 31, 32 to 63, ...) at most 2 rows name the same one
- block_tile: int32 [8192, 2], P(('grp', 'gz')), may hold values from 0 to 31
Outputs:
- marker_velocity: float32 [8192, 3, 256], P(('grp', 'gz'))
Inputs may be any that keep to these rules, and one draw needn't show every extreme that they name: marker_offsets[b, 0, m] is 0 or 1; the other two entries run from 0 to 8. `block_source`: the rows of one device name one index at most 2 times.
All inputs are finite; a program needn't handle non-finite values.
Results may differ from a plain program's by a relative error of at most 0.0003.
Values sent between devices are 32-bit elements; how exact they have to be, the bound alone decides.
A program may use at most 320 MiB of HBM per device.

v0:
```python
import functools
import math

import jax
import jax.numpy as jnp
import ml_dtypes
import numpy as np
from jax import lax
from jax.experimental import pallas as pl
from jax.experimental.pallas import tpu as pltpu
from jax.sharding import PartitionSpec as P

MESH = pl.DeviceIdType.MESH
REACH = 2
PLANES = 2 * REACH + 1
CELLS = 12
LANES = 128
ROWS_OUT = 40


def bit_reversed(count):
    bits = count.bit_length() - 1
    return np.array([int(format(i, f"0{bits}b")[::-1], 2) if bits else 0 for i in range(count)])


def split_table(values):
    high = values.astype(ml_dtypes.bfloat16)
    low = (values - high.astype(np.float64)).astype(ml_dtypes.bfloat16)
    return jnp.asarray(high), jnp.asarray(low)


def split(x):
    high = x.astype(jnp.bfloat16)
    return high, (x - high.astype(jnp.float32)).astype(jnp.bfloat16)


def dot(a, b):
    return jnp.dot(a, b, preferred_element_type=jnp.float32)


def dot3(a, b):
    return dot(a[0], b[0]) + (dot(a[1], b[0]) + dot(a[0], b[1]))


def turn(re, im, angle_num, angle_den):
    eighth = 8 * angle_num % (8 * angle_den) / angle_den
    if eighth == 0:
        return re, im
    if eighth == 2:
        return -im, re
    cosine, sine = math.cos(math.pi * eighth / 4), math.sin(math.pi * eighth / 4)
    if eighth == 1:
        return (re - im) * cosine, (re + im) * cosine
    if eighth == 3:
        return (re + im) * cosine, (re - im) * sine
    return cosine * re - sine * im, sine * re + cosine * im


def butterflies(items, first_half, position_of, real_at_end=False):
    count = len(items)
    half = 1
    while half < count:
        last = real_at_end and 2 * half == count
        for low in range(count):
            if low // half % 2:
                continue
            high = low + half
            span = half * first_half
            re, im = turn(*items[high], position_of(low) % span, 2 * span)
            first = items[low]
            if last:
                items[low], items[high] = (first[0] + re, None), (first[0] - re, None)
            else:
                items[low] = (first[0] + re, first[1] + im)
                items[high] = (first[0] - re, first[1] - im)
        half *= 2
    return items


def wait_for(ref, semaphore):
    pltpu.make_async_copy(ref, ref, semaphore).wait()


def transform_kernel(
    groups,
    slabs,
    spec_ref,
    cos_hi,
    cos_lo,
    sin_hi,
    sin_lo,
    twiddle_ref,
    out_ref,
    plane_t,
    rows_in,
    rows_z,
    ring_in,
    real_z,
    velocity,
    send_a,
    recv_a,
    send_b,
    recv_b,
    send_c,
    recv_c,
):
    g = lax.axis_index("grp")
    s = lax.axis_index("gz")
    side = spec_ref.shape[2]
    rows = side // slabs
    share = slabs // groups
    components = spec_ref.shape[1]

    barrier = pltpu.get_barrier_semaphore()

    def greet_slab(i, carry):
        pl.semaphore_signal(barrier, inc=1, device_id=(g, lax.rem(s + i, slabs)), device_id_type=MESH)
        return carry

    def greet_ring(i, carry):
        pl.semaphore_signal(barrier, inc=1, device_id=(lax.rem(g + i, groups), s), device_id_type=MESH)
        return carry

    lax.fori_loop(1, slabs, greet_slab, 0)
    lax.fori_loop(1, groups, greet_ring, 0)

    def transform_plane(c):
        cosine, sine = (cos_hi[...], cos_lo[...]), (sin_hi[...], sin_lo[...])
        re, im = split(spec_ref[0, c]), split(spec_ref[1, c])
        row_re = split(dot3(re, cosine) - dot3(im, sine))
        row_im = split(dot3(re, sine) + dot3(im, cosine))
        plane_t[c, 0] = dot3(cosine, row_re) - dot3(sine, row_im)
        plane_t[c, 1] = dot3(sine, row_re) + dot3(cosine, row_im)

    def send_rows(c):
        def one(i, carry):
            r = lax.rem(s + i, slabs)
            pltpu.make_async_remote_copy(
                src_ref=plane_t.at[c, :, pl.ds(pl.multiple_of(r * rows, rows), rows), :],
                dst_ref=rows_in.at[c, s],
                send_sem=send_a.at[c],
                recv_sem=recv_a.at[c],
                device_id=(g, r),
                device_id_type=MESH,
            ).start()
            return carry

        pltpu.make_async_copy(
            plane_t.at[c, :, pl.ds(pl.multiple_of(s * rows, rows), rows), :],
            rows_in.at[c, s],
            recv_a.at[c],
        ).start()
        lax.fori_loop(1, slabs, one, 0)

    transform_plane(0)
    pl.semaphore_wait(barrier, slabs - 1 + groups - 1)
    send_rows(0)

    def later_plane(c, carry):
        transform_plane(c)
        send_rows(c)
        return carry

    lax.fori_loop(1, components, later_plane, 0)

    inner = min(8, slabs)
    outer = slabs // inner

    def along_slab(c, carry):
        wait_for(rows_in.at[c], recv_a.at[c])
        for block in range(outer):
            items = {k: (rows_in[c, inner * block + k, 0], rows_in[c, inner * block + k, 1]) for k in range(inner)}
            items = butterflies(items, 1, lambda k: k)
            for k in range(inner):
                rows_in[c, inner * block + k, 0], rows_in[c, inner * block + k, 1] = items[k]
        for k in range(inner):
            items = {m: (rows_in[c, inner * m + k, 0], rows_in[c, inner * m + k, 1]) for m in range(outer)}
            items = butterflies(items, inner, lambda m, k=k: inner * m + k)
            for m in range(outer):
                w = inner * m + k
                cosine, sine = twiddle_ref[g * 2 * slabs + 2 * w], twiddle_ref[g * 2 * slabs + 2 * w + 1]
                re, im = items[m]
                rows_z[c, w, 0] = cosine * re - sine * im
                rows_z[c, w, 1] = sine * re + cosine * im

        def one(i, inner_carry):
            to = lax.rem(g + i, groups)
            pltpu.make_async_remote_copy(
                src_ref=rows_z.at[c, pl.ds(to * share, share)],
                dst_ref=ring_in.at[c, g],
                send_sem=send_b.at[c],
                recv_sem=recv_b.at[c],
                device_id=(to, s),
                device_id_type=MESH,
            ).start()
            return inner_carry

        pltpu.make_async_copy(rows_z.at[c, pl.ds(g * share, share)], ring_in.at[c, g], recv_b.at[c]).start()
        lax.fori_loop(1, groups, one, 0)
        return carry

    lax.fori_loop(0, components, along_slab, 0)

    def along_ring(c, carry):
        wait_for(ring_in.at[c], recv_b.at[c])
        for k in range(share):
            items = {q: (ring_in[c, q, k, 0], ring_in[c, q, k, 1]) for q in range(groups)}
            items = butterflies(items, 1, lambda q: q, real_at_end=True)
            for u in range(groups):
                real_z[c, u, k] = items[u][0]

        def one(i, inner_carry):
            to = lax.rem(g + lax.div(i, share), groups)
            k = lax.rem(i, share)
            w = g * share + k
            mine = jnp.logical_and(to == g, w == s)
            place = velocity.at[c, pl.ds(pl.multiple_of(s * rows, rows), rows), :]

            @pl.when(mine)
            def _():
                pltpu.make_async_copy(real_z.at[c, to, k], place, recv_c.at[c]).start()

            @pl.when(jnp.logical_not(mine))
            def _():
                pltpu.make_async_remote_copy(
                    src_ref=real_z.at[c, to, k],
                    dst_ref=place,
                    send_sem=send_c.at[c],
                    recv_sem=recv_c.at[c],
                    device_id=(to, w),
                    device_id_type=MESH,
                ).start()

            return inner_carry

        lax.fori_loop(0, slabs, one, 0)
        return carry

    lax.fori_loop(0, components, along_ring, 0)

    def finish(c, carry):
        wait_for(velocity.at[c], recv_c.at[c])
        for half in range(side // LANES):
            columns = slice(half * LANES, (half + 1) * LANES)
            out_ref[c, half, REACH : REACH + side, :] = velocity[c, :, columns]
            out_ref[c, half, 0:REACH, :] = velocity[c, side - REACH : side, columns]
            out_ref[c, half, side + REACH : side + 8, :] = velocity[c, 0 : 8 - REACH, columns]
        return carry

    lax.fori_loop(0, components, finish, 0)

    holds_own = lax.div(s, share) == g

    def drain(c, carry):
        wait_for(rows_in.at[c, pl.ds(0, slabs - 1)], send_a.at[c])
        wait_for(ring_in.at[c, pl.ds(0, groups - 1)], send_b.at[c])

        @pl.when(holds_own)
        def _():
            wait_for(velocity.at[c, pl.ds(0, side - rows)], send_c.at[c])

        @pl.when(jnp.logical_not(holds_own))
        def _():
            wait_for(velocity.at[c], send_c.at[c])

        return carry

    lax.fori_loop(0, components, drain, 0)


def synthesize(spectrum, groups, slabs):
    components, side = spectrum.shape[1], spectrum.shape[3]
    rows, share = side // slabs, slabs // groups
    ids = np.arange(side)
    angle = 2.0 * np.pi / side * (ids[:, None] * ids[None, :] % side)
    tables = split_table(np.cos(angle)) + split_table(np.sin(angle))
    count = groups * slabs
    twist = 2.0 * np.pi / count * (bit_reversed(groups)[:, None] * np.arange(slabs)[None, :])
    scale = 1.0 / math.sqrt(side * side * count)
    twiddle = np.stack([np.cos(twist), np.sin(twist)], axis=-1) * scale
    twiddle = jnp.asarray(twiddle.reshape(-1).astype(np.float32))
    vmem = pl.BlockSpec(memory_space=pltpu.VMEM)
    f32 = jnp.float32
    return pl.pallas_call(
        functools.partial(transform_kernel, groups, slabs),
        out_shape=jax.ShapeDtypeStruct((components, side // LANES, side + 8, LANES), f32),
        in_specs=[vmem] * 5 + [pl.BlockSpec(memory_space=pltpu.SMEM)],
        out_specs=vmem,
        scratch_shapes=[
            pltpu.VMEM((components, 2, side, side), f32),
            pltpu.VMEM((components, slabs, 2, rows, side), f32),
            pltpu.VMEM((components, slabs, 2, rows, side), f32),
            pltpu.VMEM((components, groups, share, 2, rows, side), f32),
            pltpu.VMEM((components, groups, share, rows, side), f32),
            pltpu.VMEM((components, side, side), f32),
        ]
        + [pltpu.SemaphoreType.DMA((components,))] * 6,
        compiler_params=pltpu.CompilerParams(
            collective_id=0, has_side_effects=True, vmem_limit_bytes=40 * 2**20
        ),
        cost_estimate=pl.CostEstimate(flops=2_500_000_000, bytes_accessed=100_000_000, transcendentals=0),
    )(spectrum[:, :, 0], *tables, twiddle)


def cut_kernel(plane_ref, request_ref, message_ref):
    slabs = message_ref.shape[0]
    lane = lax.broadcasted_iota(jnp.int32, (16, LANES), 1)
    low_half = lax.broadcasted_iota(jnp.int32, (8, LANES), 0) < 4

    def serve(home, carry):
        cut = [jnp.zeros((16, LANES), jnp.float32) for _ in range(3)]
        for slot in range(2 * PLANES):
            start = pl.multiple_of(request_ref[(slot * slabs + home) * 2], 8)
            first = request_ref[(slot * slabs + home) * 2 + 1]
            half = first >> 7
            first = first & (LANES - 1)
            taken = jnp.logical_and(lane >= CELLS * slot, lane < CELLS * (slot + 1))
            near = lane >= first
            for c in range(3):
                cells = jnp.where(
                    near,
                    plane_ref[c, half, pl.ds(start, 16), :],
                    plane_ref[c, 1 - half, pl.ds(start, 16), :],
                )
                moved = pltpu.roll(cells, (CELLS * slot + LANES - first) & (LANES - 1), 1)
                cut[c] = jnp.where(taken, moved, cut[c])
        for c in range(3):
            message_ref[home, 8 * c : 8 * c + 8, :] = cut[c][0:8]
        message_ref[home, 24:32, :] = jnp.where(low_half, cut[0][8:16], pltpu.roll(cut[1][8:16], 4, 0))
        message_ref[home, 32:40, :] = cut[2][8:16]
        return carry

    lax.fori_loop(0, slabs, serve, 0)


def exchange_kernel(groups, slabs, message, inbox, send_sem, edge_sem, recv_sem):
    g = lax.axis_index("grp")
    s = lax.axis_index("gz")
    below, above = lax.rem(g + groups - 1, groups), lax.rem(g + 1, groups)
    at_start, at_end = s < REACH, s >= slabs - REACH
    at_edge = jnp.logical_or(at_start, at_end)

    barrier = pltpu.get_barrier_semaphore()

    def greet_slab(i, carry):
        pl.semaphore_signal(barrier, inc=1, device_id=(g, lax.rem(s + i, slabs)), device_id_type=MESH)
        return carry

    lax.fori_loop(1, slabs, greet_slab, 0)
    for k in range(REACH):
        pl.semaphore_signal(barrier, inc=1, device_id=(below, slabs - 1 - k), device_id_type=MESH)
        pl.semaphore_signal(barrier, inc=1, device_id=(above, k), device_id_type=MESH)

    @pl.when(at_edge)
    def _():
        pl.semaphore_wait(barrier, 2 * slabs - 1)

    @pl.when(jnp.logical_not(at_edge))
    def _():
        pl.semaphore_wait(barrier, slabs - 1)

    edge_group = jnp.where(at_start, below, above)
    edge_place = jnp.where(at_start, slabs + REACH + s, s - (slabs - REACH))

    def send(i, carry):
        home = lax.rem(s + i, slabs)

        @pl.when(at_edge)
        def _():
            pltpu.make_async_remote_copy(
                src_ref=message.at[home],
                dst_ref=inbox.at[edge_place],
                send_sem=edge_sem,
                recv_sem=recv_sem,
                device_id=(edge_group, home),
                device_id_type=MESH,
            ).start()

        @pl.when(i == 0)
        def _():
            pltpu.make_async_copy(message.at[home], inbox.at[REACH + s], recv_sem).start()

        @pl.when(i > 0)
        def _():
            pltpu.make_async_remote_copy(
                src_ref=message.at[home],
                dst_ref=inbox.at[REACH + s],
                send_sem=send_sem,
                recv_sem=recv_sem,
                device_id=(g, home),
                device_id_type=MESH,
            ).start()

        return carry

    lax.fori_loop(0, slabs, send, 0)
    wait_for(inbox, recv_sem)
    wait_for(inbox.at[pl.ds(0, slabs - 1)], send_sem)

    @pl.when(at_edge)
    def _():
        wait_for(inbox.at[pl.ds(0, slabs)], edge_sem)


def interpolate_kernel(inbox, home_ref, fraction_ref, offset_ref, out_ref, weights):
    blocks, markers = fraction_ref.shape[0], fraction_ref.shape[2]
    weights[...] = jnp.zeros_like(weights)
    row_y = lax.broadcasted_iota(jnp.int32, (16, markers), 0)
    row_x = jnp.where(row_y < 12, row_y, row_y - 4)
    in_low = lax.broadcasted_iota(jnp.int32, (8, markers), 0) < 4

    def interpolate(i, carry):
        f = fraction_ref[i]
        o = offset_ref[i]
        root = jnp.sqrt(1.0 + 4.0 * f - 4.0 * f * f)
        low, high = 3.0 - 2.0 * f, 1.0 + 2.0 * f
        taps = ((low - root) * 0.125, (low + root) * 0.125, (high + root) * 0.125, (high - root) * 0.125)
        weight_x = jnp.zeros((16, markers), jnp.float32)
        weight_y = jnp.zeros((16, markers), jnp.float32)
        for e in range(4):
            weight_x = jnp.where(row_x == o[1:2] + e, taps[e][1:2], weight_x)
            weight_y = jnp.where(row_y == o[2:3] + e, taps[e][2:3], weight_y)
        y_high, y_low = split(weight_y)
        weights[0, 0:16, :] = y_high
        weights[1, 0:16, :] = y_low
        near = o[0:1] == 0
        none = jnp.zeros((1, markers), jnp.float32)
        tap_z = [none] + [tap[0:1] for tap in taps] + [none]
        weight_z = [jnp.where(near, tap_z[j + 1], tap_z[j]) for j in range(PLANES)]
        source = home_ref[i]
        slot = home_ref[blocks + i]
        cells = []
        for j in range(PLANES):
            place = CELLS * (2 * (PLANES - 1 - j) + slot)
            cells.append(pltpu.roll(inbox[source + j], (2 * LANES - place) & (LANES - 1), 1))
        cells_high, cells_low = split(jnp.concatenate(cells, axis=0))
        values = dot(cells_high, weights[0]) + (dot(cells_low, weights[0]) + dot(cells_high, weights[1]))
        sums = []
        for t in range(ROWS_OUT // 8):
            total = weight_z[0] * values[8 * t : 8 * t + 8]
            for j in range(1, PLANES):
                total = total + weight_z[j] * values[ROWS_OUT * j + 8 * t : ROWS_OUT * j + 8 * t + 8]
            sums.append(total)
        x_first, x_last = weight_x[0:8], weight_x[8:16]
        mixed, last = sums[3] * x_last, sums[4] * x_last
        tails = (jnp.where(in_low, mixed, 0.0), jnp.where(in_low, 0.0, mixed), jnp.where(in_low, last, 0.0))
        for c in range(3):
            out_ref[i, c : c + 1, :] = jnp.sum(sums[c] * x_first + tails[c], axis=0, keepdims=True)
        return carry

    lax.fori_loop(0, blocks, interpolate, 0)


def sample(plane, requests, home, fraction, offsets, groups, slabs):
    vmem, smem = pl.BlockSpec(memory_space=pltpu.VMEM), pl.BlockSpec(memory_space=pltpu.SMEM)
    anywhere = pl.BlockSpec(memory_space=pl.ANY)
    markers = fraction.shape[2]
    message = pl.pallas_call(
        cut_kernel,
        out_shape=jax.ShapeDtypeStruct((slabs, ROWS_OUT, LANES), jnp.float32),
        in_specs=[vmem, smem],
        out_specs=vmem,
        cost_estimate=pl.CostEstimate(flops=5_000_000, bytes_accessed=1_500_000, transcendentals=0),
    )(plane, requests)
    inbox = pl.pallas_call(
        functools.partial(exchange_kernel, groups, slabs),
        out_shape=jax.ShapeDtypeStruct((slabs + 2 * REACH, ROWS_OUT, LANES), jnp.float32),
        in_specs=[anywhere],
        out_specs=anywhere,
        scratch_shapes=[pltpu.SemaphoreType.DMA] * 3,
        compiler_params=pltpu.CompilerParams(collective_id=1, has_side_effects=True),
        cost_estimate=pl.CostEstimate(flops=0, bytes_accessed=20_000_000, transcendentals=0),
    )(message)
    return pl.pallas_call(
        interpolate_kernel,
        out_shape=jax.ShapeDtypeStruct(fraction.shape, jnp.float32),
        in_specs=[vmem, smem, vmem, vmem],
        out_specs=vmem,
        scratch_shapes=[pltpu.VMEM((2, LANES, markers), jnp.bfloat16)],
        cost_estimate=pl.CostEstimate(flops=200_000_000, bytes_accessed=1_500_000, transcendentals=25_000),
    )(inbox, home, fraction, offsets)


def patch_requests(block_source, block_tile, groups, slabs, side):
    asked = jnp.concatenate([block_source, block_tile], axis=1)
    everyone = lax.all_gather(asked, ("grp", "gz"), axis=0, tiled=False)
    blocks = block_source.shape[0]
    everyone = everyone.reshape(groups, slabs, blocks, 3)
    position = lax.axis_index("grp") * slabs + lax.axis_index("gz")
    count = groups * slabs
    order = jnp.arange(blocks, dtype=jnp.int32)
    requests = []
    for step in range(-REACH, REACH + 1):
        centre = (position + step + count) % count
        near = lax.dynamic_index_in_dim(everyone, centre // slabs, 0, keepdims=False)
        named = near[:, :, 0] == centre % slabs
        code = (order[None, :] * side + near[:, :, 1]) * side + near[:, :, 2]
        first = jnp.min(jnp.where(named, code, side * side * blocks), axis=1)
        second = jnp.max(jnp.where(named, code, 0), axis=1)
        for chosen in (first, second):
            tile_x, tile_y = chosen // side % side, chosen % side
            requests.append(jnp.stack([8 * tile_x, (8 * tile_y - 2 + side) % side], axis=-1))
    return jnp.stack(requests).reshape(-1)


def local(groups, slabs, spectrum, marker_fraction, marker_offsets, block_source, block_tile):
    side = spectrum.shape[3]
    requests = patch_requests(block_source, block_tile, groups, slabs, side)
    source = block_source[:, 0]
    order = jnp.arange(source.shape[0])
    again = jnp.any((source[:, None] == source[None, :]) & (order[:, None] > order[None, :]), axis=1)
    home = jnp.concatenate([source, again.astype(jnp.int32)])
    plane = synthesize(spectrum, groups, slabs)
    return sample(plane, requests, home, marker_fraction, marker_offsets, groups, slabs)


def solution(mesh):
    groups, slabs = mesh.shape["grp"], mesh.shape["gz"]
    both = ("grp", "gz")
    return jax.shard_map(
        functools.partial(local, groups, slabs),
        mesh=mesh,
        in_specs=(
            P(None, None, both, None, None),
            P(both, None, None),
            P(both, None, None),
            P(both, None),
            P(both, None),
        ),
        out_specs=P(both, None, None),
        check_vma=False,
    )
```

profile of v0, /device:TPU:1, one launch (start us, length us, event | category | flops | bytes accessed | tf_op | source)
XLA Modules:
  0.0 188.4 jit_solution(6779417300122785448)
XLA Ops:
  0.0 0.0 copy-start.2
  0.0 0.0 copy-start.3
  0.0 0.0 copy-start.4
  0.0 0.0 copy-start.5
  0.0 0.0 copy-start.6
  0.0 0.0 copy-start.1
  0.3 0.9 add_bitcast_fusion
  1.2 73.0 %all-gather.1 = s32[256,32,3]{1,2,0:T(4,128)S(1)} all-gather(s32[1,32,3]{1,2,0:T(4,128)S(1)} %add_bitcast_fusion), channel_id=2, replica_groups=mesh['grp'=8,'gz'=32] {'grp','gz'}, dimensions={0}, use_global_device_ids=true | all-gather | bytes 98688 | tf_op jit(solution)/shard_map/all_gather | solution.py:486
  74.1 0.1 constant_dynamic-slice_fusion.2
  74.3 0.3 select_reduce_fusion
  74.9 0.1 copy.44
  75.0 0.7 reshape.1493.request_ref
  75.7 0.0 copy-done.2
  75.7 0.0 copy-done.3
  75.7 0.0 copy-done.4
  75.7 0.0 copy-done.5
  75.7 0.0 copy-done.6
  75.8 0.0 copy-done.1
  75.8 65.3 %shard_map.100.plane_ref = f32[3,2,264,128]{3,2,1,0:T(8,128)S(1)} custom-call(f32[2,3,256,256]{3,2,1,0:T(8,128)S(1)} %bitcast.348, bf16[256,256]{1,0:T(8,128)(2,1)S(1)} %copy-done.2, bf16[256,256]{1,0:T(8,128)(2,1)S(1)} %copy-done.3, bf16[256,256]{1,0:T(8,128)(2,1)S(1)} %copy-done.4, bf16[256,256]{1,0:T(8,128)(2,1)S(1)} %copy-done.5, f32[512]{0:T(512)S(1)} %copy-done.6), custom_call_target="tpu_custom_call" | custom-call | flops 2500000000 | bytes 100000000 | tf_op jit(solution)/shard_map/pallas_call | solution.py:284
  141.1 0.0 copy-start
  141.1 0.9 copy-done
  142.0 0.0 copy-start.9
  142.0 0.0 copy-start.7
  142.0 0.0 copy-start.8
  142.0 6.5 %shard_map.101.message = f32[32,40,128]{2,1,0:T(8,128)} custom-call(f32[3,2,264,128]{3,2,1,0:T(8,128)} %copy-done, s32[640]{0:T(1024)} %reshape.1493.request_ref), custom_call_target="tpu_custom_call" | custom-call | flops 5000000 | bytes 1500000 | tf_op jit(solution)/shard_map/pallas_call | solution.py:458
  148.5 24.3 %shard_map.102.inbox = f32[36,40,128]{2,1,0:T(8,128)} custom-call(f32[32,40,128]{2,1,0:T(8,128)} %shard_map.101.message), custom_call_target="tpu_custom_call" | custom-call | bytes 20000000 | tf_op jit(solution)/shard_map/pallas_call | solution.py:465
  172.8 0.0 copy-done.9
  172.8 0.2 fusion.16
  173.0 0.6 pad_add_fusion.home_ref
  173.6 0.0 copy-done.7
  173.6 0.7 copy.45.fraction_ref
  174.3 0.0 copy-done.8
  174.3 0.7 copy.46.offset_ref
  175.0 11.8 %shard_map.103 = f32[32,3,256]{2,1,0:T(4,128)} custom-call(f32[36,40,128]{2,1,0:T(8,128)} %shard_map.102.inbox, s32[64]{0:T(128)} %pad_add_fusion.home_ref, f32[32,3,256]{2,1,0:T(4,128)} %copy.45.fraction_ref, s32[32,3,256]{2,1,0:T(4,128)} %copy.46.offset_ref), custom_call_target="tpu_custom_call" | custom-call | flops 200000000 | bytes 1500000 | tf_op jit(solution)/shard_map/pallas_call | solution.py:474
  186.8 1.6 copy.47
  (22 shorter events, 0.3 us)
Async XLA Ops:
  0.0 75.7 %copy-start.2 = (bf16[256,256]{1,0:T(8,128)(2,1)S(1)}, bf16[256,256]{1,0:T(8,128)(2,1)}, u32[]{:S(2)}) copy-start(bf16[256,256]{1,0:T(8,128)(2,1)} %constant.399.clone.cos_hi) | copy-start | bytes 393220
  0.0 75.7 %copy-start.3 = (bf16[256,256]{1,0:T(8,128)(2,1)S(1)}, bf16[256,256]{1,0:T(8,128)(2,1)}, u32[]{:S(2)}) copy-start(bf16[256,256]{1,0:T(8,128)(2,1)} %constant.400.clone.cos_lo) | copy-start | bytes 393220
  0.0 75.7 %copy-start.4 = (bf16[256,256]{1,0:T(8,128)(2,1)S(1)}, bf16[256,256]{1,0:T(8,128)(2,1)}, u32[]{:S(2)}) copy-start(bf16[256,256]{1,0:T(8,128)(2,1)} %constant.401.clone.sin_hi) | copy-start | bytes 393220
  0.0 75.7 %copy-start.5 = (bf16[256,256]{1,0:T(8,128)(2,1)S(1)}, bf16[256,256]{1,0:T(8,128)(2,1)}, u32[]{:S(2)}) copy-start(bf16[256,256]{1,0:T(8,128)(2,1)} %constant.402.clone.sin_lo) | copy-start | bytes 393220
  0.0 75.7 %copy-start.6 = (f32[512]{0:T(512)S(1)}, f32[512]{0:T(512)}, u32[]{:S(2)}) copy-start(f32[512]{0:T(512)} %constant.403.clone.twiddle_ref) | copy-start | bytes 6148
  0.0 75.7 %copy-start.1 = (f32[2,3,1,256,256]{4,3,2,1,0:T(8,128)S(1)}, f32[2,3,1,256,256]{4,3,2,1,0:T(8,128)}, u32[]{:S(2)}) copy-start(f32[2,3,1,256,256]{4,3,2,1,0:T(8,128)} %param.10) | copy-start | bytes 4718596
  141.1 0.9 copy-start
  142.0 30.8 %copy-start.9 = (s32[32,1]{0,1:T(1,128)S(1)}, s32[32,1]{0,1:T(1,128)}, u32[]{:S(2)}) copy-start(s32[32,1]{0,1:T(1,128)} %param.13) | copy-start | bytes 388
  142.0 31.6 %copy-start.7 = (f32[32,3,256]{2,0,1:T(8,128)S(1)}, f32[32,3,256]{2,0,1:T(8,128)}, u32[]{:S(2)}) copy-start(f32[32,3,256]{2,0,1:T(8,128)} %param.11) | copy-start | bytes 294916
  142.0 32.3 %copy-start.8 = (s32[32,3,256]{2,0,1:T(8,128)S(1)}, s32[32,3,256]{2,0,1:T(8,128)}, u32[]{:S(2)}) copy-start(s32[32,3,256]{2,0,1:T(8,128)} %param.12) | copy-start | bytes 294916
where the time goes:
time: 189 us; the launch traced here: 188 us
  Pallas kernels  108 us (57%)
  blocking collectives  73 us (39%)
  local copies, waits for them, and re-layouts  4.88 us (3%)
  other arithmetic  2.23 us (1%)
    all_gather x1, blocking collectives, patch_requests(): everyone = lax.all_gather(asked, ('grp', 'gz'), axis=0, tiled=False)  73 us
    pallas_call x1, Pallas kernels, synthesize(): pl.pallas_call(functools.partial(transform_kernel, groups, slabs), out_sh...  65.3 us
    pallas_call x1, Pallas kernels, sample(): pl.pallas_call(functools.partial(exchange_kernel, groups, slabs), out_sha...  24.3 us
    pallas_call x1, Pallas kernels, sample(): pl.pallas_call(interpolate_kernel, out_shape=jax.ShapeDtypeStruct(fractio...  11.8 us
    pallas_call x1, Pallas kernels, sample(): pl.pallas_call(cut_kernel, out_shape=jax.ShapeDtypeStruct((slabs, ROWS_OU...  6.49 us

commit v1 on v0

--- a/solution.py
+++ b/solution.py
@@ -81,9 +81,14 @@
     pltpu.make_async_copy(ref, ref, semaphore).wait()
 
 
+def nearby(me, i, count):
+    return lax.rem(me + (2 * lax.rem(i, 2) - 1) * lax.div(i + 1, 2) + count, count)
+
+
 def transform_kernel(
     groups,
     slabs,
+    asking_ref,
     spec_ref,
     cos_hi,
     cos_lo,
@@ -91,6 +96,7 @@
     sin_lo,
     twiddle_ref,
     out_ref,
+    asked_ref,
     plane_t,
     rows_in,
     rows_z,
@@ -103,6 +109,8 @@
     recv_b,
     send_c,
     recv_c,
+    send_q,
+    recv_q,
 ):
     g = lax.axis_index("grp")
     s = lax.axis_index("gz")
@@ -111,18 +119,32 @@
     share = slabs // groups
     components = spec_ref.shape[1]
 
+    below, above = lax.rem(g + groups - 1, groups), lax.rem(g + 1, groups)
+    at_start, at_end = s < REACH, s >= slabs - REACH
+    at_edge = jnp.logical_or(at_start, at_end)
+    edge_group = jnp.where(at_start, below, above)
+
     barrier = pltpu.get_barrier_semaphore()
 
     def greet_slab(i, carry):
         pl.semaphore_signal(barrier, inc=1, device_id=(g, lax.rem(s + i, slabs)), device_id_type=MESH)
         return carry
 
+    def greet_edge(i, carry):
+        pl.semaphore_signal(barrier, inc=1, device_id=(edge_group, lax.rem(s + i, slabs)), device_id_type=MESH)
+        return carry
+
     def greet_ring(i, carry):
         pl.semaphore_signal(barrier, inc=1, device_id=(lax.rem(g + i, groups), s), device_id_type=MESH)
         return carry
 
     lax.fori_loop(1, slabs, greet_slab, 0)
     lax.fori_loop(1, groups, greet_ring, 0)
+
+    @pl.when(at_edge)
+    def _():
+        lax.fori_loop(0, slabs, greet_edge, 0)
+
 
     def transform_plane(c):
         cosine, sine = (cos_hi[...], cos_lo[...]), (sin_hi[...], sin_lo[...])
@@ -134,7 +156,7 @@
 
     def send_rows(c):
         def one(i, carry):
-            r = lax.rem(s + i, slabs)
+            r = nearby(s, i, slabs)
             pltpu.make_async_remote_copy(
                 src_ref=plane_t.at[c, :, pl.ds(pl.multiple_of(r * rows, rows), rows), :],
                 dst_ref=rows_in.at[c, s],
@@ -152,9 +174,28 @@
         ).start()
         lax.fori_loop(1, slabs, one, 0)
 
+    def ask(place, device):
+        pltpu.make_async_remote_copy(
+            src_ref=asking_ref,
+            dst_ref=asked_ref.at[place],
+            send_sem=send_q,
+            recv_sem=recv_q,
+            device_id=device,
+            device_id_type=MESH,
+        ).start()
+
+    def ask_slab(i, carry):
+        ask(s, (g, nearby(s, i, slabs)))
+        return carry
+
     transform_plane(0)
-    pl.semaphore_wait(barrier, slabs - 1 + groups - 1)
+    pl.semaphore_wait(barrier, slabs - 1 + groups - 1 + 2 * REACH)
     send_rows(0)
+    pltpu.make_async_copy(asking_ref, asked_ref.at[s], recv_q).start()
+    lax.fori_loop(1, slabs, ask_slab, 0)
+    for k in range(REACH):
+        ask(slabs + s, (below, slabs - 1 - k))
+        ask(slabs + s, (above, k))
 
     def later_plane(c, carry):
         transform_plane(c)
@@ -184,7 +225,7 @@
                 rows_z[c, w, 1] = sine * re + cosine * im
 
         def one(i, inner_carry):
-            to = lax.rem(g + i, groups)
+            to = nearby(g, i, groups)
             pltpu.make_async_remote_copy(
                 src_ref=rows_z.at[c, pl.ds(to * share, share)],
                 dst_ref=ring_in.at[c, g],
@@ -210,7 +251,7 @@
                 real_z[c, u, k] = items[u][0]
 
         def one(i, inner_carry):
-            to = lax.rem(g + lax.div(i, share), groups)
+            to = nearby(g, lax.div(i, share), groups)
             k = lax.rem(i, share)
             w = g * share + k
             mine = jnp.logical_and(to == g, w == s)
@@ -249,6 +290,16 @@
 
     lax.fori_loop(0, components, finish, 0)
 
+    @pl.when(at_edge)
+    def _():
+        wait_for(asked_ref, recv_q)
+
+    @pl.when(jnp.logical_not(at_edge))
+    def _():
+        wait_for(asked_ref.at[pl.ds(0, slabs)], recv_q)
+
+    wait_for(asked_ref.at[pl.ds(0, slabs - 1 + 2 * REACH)], send_q)
+
     holds_own = lax.div(s, share) == g
 
     def drain(c, carry):
@@ -268,7 +319,7 @@
     lax.fori_loop(0, components, drain, 0)
 
 
-def synthesize(spectrum, groups, slabs):
+def synthesize(asking, spectrum, groups, slabs):
     components, side = spectrum.shape[1], spectrum.shape[3]
     rows, share = side // slabs, slabs // groups
     ids = np.arange(side)
@@ -283,9 +334,12 @@
     f32 = jnp.float32
     return pl.pallas_call(
         functools.partial(transform_kernel, groups, slabs),
-        out_shape=jax.ShapeDtypeStruct((components, side // LANES, side + 8, LANES), f32),
-        in_specs=[vmem] * 5 + [pl.BlockSpec(memory_space=pltpu.SMEM)],
-        out_specs=vmem,
+        out_shape=(
+            jax.ShapeDtypeStruct((components, side // LANES, side + 8, LANES), f32),
+            jax.ShapeDtypeStruct((2 * slabs, 1, LANES), jnp.int32),
+        ),
+        in_specs=[vmem] * 6 + [pl.BlockSpec(memory_space=pltpu.SMEM)],
+        out_specs=(vmem, vmem),
         scratch_shapes=[
             pltpu.VMEM((components, 2, side, side), f32),
             pltpu.VMEM((components, slabs, 2, rows, side), f32),
@@ -294,24 +348,30 @@
             pltpu.VMEM((components, groups, share, rows, side), f32),
             pltpu.VMEM((components, side, side), f32),
         ]
-        + [pltpu.SemaphoreType.DMA((components,))] * 6,
+        + [pltpu.SemaphoreType.DMA((components,))] * 6
+        + [pltpu.SemaphoreType.DMA] * 2,
         compiler_params=pltpu.CompilerParams(
             collective_id=0, has_side_effects=True, vmem_limit_bytes=40 * 2**20
         ),
         cost_estimate=pl.CostEstimate(flops=2_500_000_000, bytes_accessed=100_000_000, transcendentals=0),
-    )(spectrum[:, :, 0], *tables, twiddle)
+    )(asking, spectrum[:, :, 0], *tables, twiddle)
 
 
 def cut_kernel(plane_ref, request_ref, message_ref):
     slabs = message_ref.shape[0]
+    s = lax.axis_index("gz")
     lane = lax.broadcasted_iota(jnp.int32, (16, LANES), 1)
     low_half = lax.broadcasted_iota(jnp.int32, (8, LANES), 0) < 4
 
     def serve(home, carry):
         cut = [jnp.zeros((16, LANES), jnp.float32) for _ in range(3)]
         for slot in range(2 * PLANES):
-            start = pl.multiple_of(request_ref[(slot * slabs + home) * 2], 8)
-            first = request_ref[(slot * slabs + home) * 2 + 1]
+            centre = s + slot // 2 - REACH
+            inside = jnp.logical_and(centre >= 0, centre < slabs)
+            row = jnp.where(inside, home, home + slabs)
+            column = 4 * lax.rem(centre + slabs, slabs) + 2 * (slot % 2)
+            start = pl.multiple_of(request_ref[row, 0, column], 8)
+            first = request_ref[row, 0, column + 1]
             half = first >> 7
             first = first & (LANES - 1)
             taken = jnp.logical_and(lane >= CELLS * slot, lane < CELLS * (slot + 1))
@@ -363,7 +423,7 @@
     edge_place = jnp.where(at_start, slabs + REACH + s, s - (slabs - REACH))
 
     def send(i, carry):
-        home = lax.rem(s + i, slabs)
+        home = nearby(s, i, slabs)
 
         @pl.when(at_edge)
         def _():
@@ -403,27 +463,27 @@
 
 
 def interpolate_kernel(inbox, home_ref, fraction_ref, offset_ref, out_ref, weights):
-    blocks, markers = fraction_ref.shape[0], fraction_ref.shape[2]
+    blocks, markers = fraction_ref.shape[1], fraction_ref.shape[2]
     weights[...] = jnp.zeros_like(weights)
     row_y = lax.broadcasted_iota(jnp.int32, (16, markers), 0)
     row_x = jnp.where(row_y < 12, row_y, row_y - 4)
     in_low = lax.broadcasted_iota(jnp.int32, (8, markers), 0) < 4
 
     def interpolate(i, carry):
-        f = fraction_ref[i]
-        o = offset_ref[i]
+        f = jnp.concatenate([fraction_ref[d, pl.ds(i, 1), :] for d in range(3)], axis=0)
+        o = [offset_ref[d, pl.ds(i, 1), :] for d in range(3)]
         root = jnp.sqrt(1.0 + 4.0 * f - 4.0 * f * f)
         low, high = 3.0 - 2.0 * f, 1.0 + 2.0 * f
         taps = ((low - root) * 0.125, (low + root) * 0.125, (high + root) * 0.125, (high - root) * 0.125)
         weight_x = jnp.zeros((16, markers), jnp.float32)
         weight_y = jnp.zeros((16, markers), jnp.float32)
         for e in range(4):
-            weight_x = jnp.where(row_x == o[1:2] + e, taps[e][1:2], weight_x)
-            weight_y = jnp.where(row_y == o[2:3] + e, taps[e][2:3], weight_y)
+            weight_x = jnp.where(row_x == o[1] + e, taps[e][1:2], weight_x)
+            weight_y = jnp.where(row_y == o[2] + e, taps[e][2:3], weight_y)
         y_high, y_low = split(weight_y)
         weights[0, 0:16, :] = y_high
         weights[1, 0:16, :] = y_low
-        near = o[0:1] == 0
+        near = o[0] == 0
         none = jnp.zeros((1, markers), jnp.float32)
         tap_z = [none] + [tap[0:1] for tap in taps] + [none]
         weight_z = [jnp.where(near, tap_z[j + 1], tap_z[j]) for j in range(PLANES)]
@@ -445,7 +505,7 @@
         mixed, last = sums[3] * x_last, sums[4] * x_last
         tails = (jnp.where(in_low, mixed, 0.0), jnp.where(in_low, 0.0, mixed), jnp.where(in_low, last, 0.0))
         for c in range(3):
-            out_ref[i, c : c + 1, :] = jnp.sum(sums[c] * x_first + tails[c], axis=0, keepdims=True)
+            out_ref[c, pl.ds(i, 1), :] = jnp.sum(sums[c] * x_first + tails[c], axis=0, keepdims=True)
         return carry
 
     lax.fori_loop(0, blocks, interpolate, 0)
@@ -453,7 +513,6 @@
 
 def sample(plane, requests, home, fraction, offsets, groups, slabs):
     vmem, smem = pl.BlockSpec(memory_space=pltpu.VMEM), pl.BlockSpec(memory_space=pltpu.SMEM)
-    anywhere = pl.BlockSpec(memory_space=pl.ANY)
     markers = fraction.shape[2]
     message = pl.pallas_call(
         cut_kernel,
@@ -465,8 +524,8 @@
     inbox = pl.pallas_call(
         functools.partial(exchange_kernel, groups, slabs),
         out_shape=jax.ShapeDtypeStruct((slabs + 2 * REACH, ROWS_OUT, LANES), jnp.float32),
-        in_specs=[anywhere],
-        out_specs=anywhere,
+        in_specs=[vmem],
+        out_specs=vmem,
         scratch_shapes=[pltpu.SemaphoreType.DMA] * 3,
         compiler_params=pltpu.CompilerParams(collective_id=1, has_side_effects=True),
         cost_estimate=pl.CostEstimate(flops=0, bytes_accessed=20_000_000, transcendentals=0),
@@ -481,37 +540,28 @@
     )(inbox, home, fraction, offsets)
 
 
-def patch_requests(block_source, block_tile, groups, slabs, side):
-    asked = jnp.concatenate([block_source, block_tile], axis=1)
-    everyone = lax.all_gather(asked, ("grp", "gz"), axis=0, tiled=False)
-    blocks = block_source.shape[0]
-    everyone = everyone.reshape(groups, slabs, blocks, 3)
-    position = lax.axis_index("grp") * slabs + lax.axis_index("gz")
-    count = groups * slabs
+def patch_requests(source, block_tile, slabs, side):
+    blocks = source.shape[0]
     order = jnp.arange(blocks, dtype=jnp.int32)
-    requests = []
-    for step in range(-REACH, REACH + 1):
-        centre = (position + step + count) % count
-        near = lax.dynamic_index_in_dim(everyone, centre // slabs, 0, keepdims=False)
-        named = near[:, :, 0] == centre % slabs
-        code = (order[None, :] * side + near[:, :, 1]) * side + near[:, :, 2]
-        first = jnp.min(jnp.where(named, code, side * side * blocks), axis=1)
-        second = jnp.max(jnp.where(named, code, 0), axis=1)
-        for chosen in (first, second):
-            tile_x, tile_y = chosen // side % side, chosen % side
-            requests.append(jnp.stack([8 * tile_x, (8 * tile_y - 2 + side) % side], axis=-1))
-    return jnp.stack(requests).reshape(-1)
+    code = (order * side + block_tile[:, 0]) * side + block_tile[:, 1]
+    named = source[None, :] == jnp.arange(slabs, dtype=jnp.int32)[:, None]
+    first = jnp.min(jnp.where(named, code[None, :], side * side * blocks), axis=1)
+    second = jnp.max(jnp.where(named, code[None, :], 0), axis=1)
+    chosen = jnp.stack([first, second], axis=1)
+    starts = jnp.stack([8 * (chosen // side % side), (8 * (chosen % side) - 2 + side) % side], axis=2)
+    return jnp.pad(starts.reshape(1, -1), ((0, 0), (0, LANES - 4 * slabs)))
 
 
 def local(groups, slabs, spectrum, marker_fraction, marker_offsets, block_source, block_tile):
-    side = spectrum.shape[3]
-    requests = patch_requests(block_source, block_tile, groups, slabs, side)
     source = block_source[:, 0]
+    asking = patch_requests(source, block_tile, slabs, spectrum.shape[3])
     order = jnp.arange(source.shape[0])
     again = jnp.any((source[:, None] == source[None, :]) & (order[:, None] > order[None, :]), axis=1)
     home = jnp.concatenate([source, again.astype(jnp.int32)])
-    plane = synthesize(spectrum, groups, slabs)
-    return sample(plane, requests, home, marker_fraction, marker_offsets, groups, slabs)
+    plane, asked = synthesize(asking, spectrum, groups, slabs)
+    fraction, offsets = jnp.transpose(marker_fraction, (1, 0, 2)), jnp.transpose(marker_offsets, (1, 0, 2))
+    answer = sample(plane, asked, home, fraction, offsets, groups, slabs)
+    return jnp.transpose(answer, (1, 0, 2))
 
 
 def solution(mesh):

time: 189 us -> 129 us (0.68)
  blocking collectives: 73 us -> 0 us
  Pallas kernels: 108 us -> 117 us
  local copies, waits for them, and re-layouts: 4.88 us -> 7.45 us
    all_gather x1 -> x0, blocking collectives: 73 us -> none  [patch_requests(): everyone = lax.all_gather(asked, ('grp', 'gz'), axis=0, tiled=False)]
    pallas_call x1, Pallas kernels: 65.3 us -> 70.6 us  [synthesize(): pl.pallas_call(functools.partial(transform_kernel, groups, slabs), out_sh...]
    unnamed x22 -> x18, local copies, waits for them, and re-layouts: 2.36 us -> 7.2 us
    pallas_call x1, Pallas kernels: 24.3 us -> 27.2 us  [sample(): pl.pallas_call(functools.partial(exchange_kernel, groups, slabs), out_sha...]
where the time goes in v1:
time: 129 us; the launch traced here: 127 us
  Pallas kernels  117 us (91%)
  local copies, waits for them, and re-layouts  7.45 us (6%)
  other arithmetic  2.33 us (2%)
    pallas_call x1, Pallas kernels, synthesize(): pl.pallas_call(functools.partial(transform_kernel, groups, slabs), out_sh...  70.6 us
    pallas_call x1, Pallas kernels, sample(): pl.pallas_call(functools.partial(exchange_kernel, groups, slabs), out_sha...  27.2 us
    pallas_call x1, Pallas kernels, sample(): pl.pallas_call(interpolate_kernel, out_shape=jax.ShapeDtypeStruct(fractio...  11.7 us
    pallas_call x1, Pallas kernels, sample(): pl.pallas_call(cut_kernel, out_shape=jax.ShapeDtypeStruct((slabs, ROWS_OU...  7.4 us
    unnamed x18, local copies, waits for them, and re-layouts  7.2 us

profile of v1, /device:TPU:1, one launch (start us, length us, event | category | flops | bytes accessed | tf_op | source)
XLA Modules:
  0.0 126.8 jit_solution(2902631481267165859)
XLA Ops:
  0.0 0.8 bitcast_add_fusion
  0.8 0.8 select_reduce_fusion.1
  1.6 0.1 copy.13
  1.7 0.1 reshape.310.asking_ref
  1.9 0.0 copy-start.2
  1.9 1.4 %copy-done.2 = f32[2,3,1,256,256]{4,3,2,1,0:T(8,128)S(1)} copy-done((f32[2,3,1,256,256]{4,3,2,1,0:T(8,128)S(1)}, f32[2,3,1,256,256]{4,3,2,1,0:T(8,128)}, u32[]{:S(2)}) %copy-start.2) | copy-done | bytes 1572888
  3.3 0.0 copy-start.3
  3.3 0.9 copy-done.3
  4.2 0.0 copy-start.4
  4.2 0.9 copy-done.4
  5.1 0.0 copy-start.5
  5.1 0.9 copy-done.5
  6.0 0.0 copy-start.6
  6.0 0.9 copy-done.6
  6.9 0.0 copy-start.7
  6.9 0.7 copy-done.7
  7.6 70.6 %shard_map.100 = (f32[3,2,264,128]{3,2,1,0:T(8,128)S(1)}, s32[64,1,128]{2,1,0:T(1,128)S(1)}) custom-call(s32[1,128]{1,0:T(1,128)S(1)} %reshape.310.asking_ref, f32[2,3,256,256]{3,2,1,0:T(8,128)S(1)} %bitcast.15, bf16[256,256]{1,0:T(8,128)(2,1)S(1)} %copy-done.3, bf16[256,256]{1,0:T(8,128)(2,1)S(1)} %copy-done.4, bf16[256,256]{1,0:T(8,128)(2,1)S(1)} %copy-done.5, ...), custom_call_target="tpu_custom_call" | custom-call | flops 2500000000 | bytes 100000000 | tf_op jit(solution)/shard_map/pallas_call | solution.py:335
  78.2 0.0 copy-start
  78.2 0.9 copy-done
  79.1 0.0 copy-start.1
  79.1 0.6 copy-done.1
  79.7 0.0 copy-start.8
  79.7 7.4 %shard_map.101.message = f32[32,40,128]{2,1,0:T(8,128)} custom-call(f32[3,2,264,128]{3,2,1,0:T(8,128)} %copy-done, s32[64,1,128]{2,1,0:T(1,128)} %copy-done.1), custom_call_target="tpu_custom_call" | custom-call | flops 5000000 | bytes 1500000 | tf_op jit(solution)/shard_map/pallas_call | solution.py:517
  87.1 27.2 %shard_map.102.inbox = f32[36,40,128]{2,1,0:T(8,128)} custom-call(f32[32,40,128]{2,1,0:T(8,128)} %shard_map.101.message), custom_call_target="tpu_custom_call" | custom-call | bytes 20000000 | tf_op jit(solution)/shard_map/pallas_call | solution.py:524
  114.3 0.0 copy-done.8
  114.3 0.2 fusion.1
  114.5 0.6 pad_add_fusion.2.home_ref
  115.1 11.7 %shard_map.103 = f32[3,32,256]{2,1,0:T(8,128)} custom-call(f32[36,40,128]{2,1,0:T(8,128)} %shard_map.102.inbox, s32[64]{0:T(128)} %pad_add_fusion.2.home_ref, f32[3,32,256]{2,1,0:T(8,128)} %bitcast.16, s32[3,32,256]{2,1,0:T(8,128)} %bitcast.17), custom_call_target="tpu_custom_call" | custom-call | flops 200000000 | bytes 1500000 | tf_op jit(solution)/shard_map/pallas_call | solution.py:533
  (4 shorter events, 0.1 us)
Async XLA Ops:
  1.9 1.4 %copy-start.2 = (f32[2,3,1,256,256]{4,3,2,1,0:T(8,128)S(1)}, f32[2,3,1,256,256]{4,3,2,1,0:T(8,128)}, u32[]{:S(2)}) copy-start(f32[2,3,1,256,256]{4,3,2,1,0:T(8,128)} %param.10) | copy-start | bytes 4718596
  3.3 0.9 copy-start.3
  4.2 0.9 copy-start.4
  5.1 0.9 copy-start.5
  6.0 0.9 copy-start.6
  6.9 0.7 copy-start.7
  78.2 0.9 copy-start
  79.1 0.6 copy-start.1
  79.7 34.6 %copy-start.8 = (s32[32,1]{0,1:T(1,128)S(1)}, s32[32,1]{0,1:T(1,128)}, u32[]{:S(2)}) copy-start(s32[32,1]{0,1:T(1,128)} %param.13) | copy-start | bytes 388

commit v2 on v1

--- a/solution.py
+++ b/solution.py
@@ -89,14 +89,16 @@
     groups,
     slabs,
     asking_ref,
+    spec_hbm,
+    table_hbm,
+    twiddle_ref,
+    inbox,
     spec_ref,
-    cos_hi,
-    cos_lo,
-    sin_hi,
-    sin_lo,
-    twiddle_ref,
-    out_ref,
+    table,
     asked_ref,
+    asked_smem,
+    padded,
+    message,
     plane_t,
     rows_in,
     rows_z,
@@ -111,10 +113,19 @@
     recv_c,
     send_q,
     recv_q,
+    load_sem,
+    table_sem,
+    send_m,
+    edge_m,
+    recv_m,
 ):
     g = lax.axis_index("grp")
     s = lax.axis_index("gz")
     side = spec_ref.shape[2]
+    loads = [pltpu.make_async_copy(table_hbm, table, table_sem)]
+    loads += [pltpu.make_async_copy(spec_hbm.at[:, c], spec_ref.at[:, c], load_sem.at[c]) for c in range(spec_ref.shape[1])]
+    for load in loads:
+        load.start()
     rows = side // slabs
     share = slabs // groups
     components = spec_ref.shape[1]
@@ -147,7 +158,8 @@
 
 
     def transform_plane(c):
-        cosine, sine = (cos_hi[...], cos_lo[...]), (sin_hi[...], sin_lo[...])
+        pltpu.make_async_copy(spec_hbm.at[:, c], spec_ref.at[:, c], load_sem.at[c]).wait()
+        cosine, sine = (table[0], table[1]), (table[2], table[3])
         re, im = split(spec_ref[0, c]), split(spec_ref[1, c])
         row_re = split(dot3(re, cosine) - dot3(im, sine))
         row_im = split(dot3(re, sine) + dot3(im, cosine))
@@ -188,6 +200,7 @@
         ask(s, (g, nearby(s, i, slabs)))
         return carry
 
+    loads[0].wait()
     transform_plane(0)
     pl.semaphore_wait(barrier, slabs - 1 + groups - 1 + 2 * REACH)
     send_rows(0)
@@ -277,26 +290,114 @@
         lax.fori_loop(0, slabs, one, 0)
         return carry
 
-    lax.fori_loop(0, components, along_ring, 0)
-
-    def finish(c, carry):
+
+    edge_place = jnp.where(at_start, slabs + REACH + s, s - (slabs - REACH))
+    low_half = lax.broadcasted_iota(jnp.int32, (8, LANES), 0) < 4
+    lane = lax.broadcasted_iota(jnp.int32, (16, LANES), 1)
+
+    def place_plane(c):
         wait_for(velocity.at[c], recv_c.at[c])
-        for half in range(side // LANES):
+        for half in range(2):
             columns = slice(half * LANES, (half + 1) * LANES)
-            out_ref[c, half, REACH : REACH + side, :] = velocity[c, :, columns]
-            out_ref[c, half, 0:REACH, :] = velocity[c, side - REACH : side, columns]
-            out_ref[c, half, side + REACH : side + 8, :] = velocity[c, 0 : 8 - REACH, columns]
-        return carry
-
-    lax.fori_loop(0, components, finish, 0)
+            whole = [velocity[c, side - REACH : side, columns], velocity[c, :, columns], velocity[c, 0 : 8 - REACH, columns]]
+            padded[c, half] = jnp.concatenate(whole, axis=0).reshape(side // 8 + 1, 8, LANES)
+
+    def cut_for(c, home):
+        cut = jnp.zeros((16, LANES), jnp.float32)
+        for slot in range(2 * PLANES):
+            centre = s + slot // 2 - REACH
+            inside = jnp.logical_and(centre >= 0, centre < slabs)
+            row = jnp.where(inside, home, home + slabs)
+            column = 4 * lax.rem(centre + slabs, slabs) + 2 * (slot % 2)
+            tile = asked_smem[row, 0, column]
+            first = asked_smem[row, 0, column + 1]
+            half = first >> 7
+            first = first & (LANES - 1)
+            near = jnp.concatenate([padded[c, half, tile], padded[c, half, tile + 1]], axis=0)
+            far = jnp.concatenate([padded[c, 1 - half, tile], padded[c, 1 - half, tile + 1]], axis=0)
+            cells = jnp.where(lane >= first, near, far)
+            moved = pltpu.roll(cells, (CELLS * slot + LANES - first) & (LANES - 1), 1)
+            taken = jnp.logical_and(lane >= CELLS * slot, lane < CELLS * (slot + 1))
+            cut = jnp.where(taken, moved, cut)
+        return cut
+
+    def deliver(home, i, tiles):
+        part = pl.ds(8 * tiles[0], 8 * len(tiles))
+
+        @pl.when(at_edge)
+        def _():
+            pltpu.make_async_remote_copy(
+                src_ref=message.at[home, part],
+                dst_ref=inbox.at[edge_place, part],
+                send_sem=edge_m,
+                recv_sem=recv_m,
+                device_id=(edge_group, home),
+                device_id_type=MESH,
+            ).start()
+
+        @pl.when(i == 0)
+        def _():
+            pltpu.make_async_copy(message.at[home, part], inbox.at[REACH + s, part], recv_m).start()
+
+        @pl.when(i > 0)
+        def _():
+            pltpu.make_async_remote_copy(
+                src_ref=message.at[home, part],
+                dst_ref=inbox.at[REACH + s, part],
+                send_sem=send_m,
+                recv_sem=recv_m,
+                device_id=(g, home),
+                device_id_type=MESH,
+            ).start()
+
+    def serve_first(i, carry):
+        home = nearby(s, i, slabs)
+        cut = cut_for(0, home)
+        message[home, 0:8, :] = cut[0:8]
+        message[home, 16:24, :] = cut[8:16]
+        return carry
+
+    def serve_second(i, carry):
+        home = nearby(s, i, slabs)
+        cut = cut_for(1, home)
+        message[home, 8:16, :] = cut[0:8]
+        message[home, 16:24, :] = jnp.where(low_half, message[home, 16:24, :], pltpu.roll(cut[8:16], 4, 0))
+        deliver(home, i, (0, 1, 2))
+        return carry
+
+    def serve_third(i, carry):
+        home = nearby(s, i, slabs)
+        message[home, 24:40, :] = cut_for(2, home)
+        deliver(home, i, (3, 4))
+        return carry
+
+    along_ring(0, 0)
 
     @pl.when(at_edge)
     def _():
         wait_for(asked_ref, recv_q)
+        pltpu.sync_copy(asked_ref, asked_smem)
 
     @pl.when(jnp.logical_not(at_edge))
     def _():
         wait_for(asked_ref.at[pl.ds(0, slabs)], recv_q)
+        pltpu.sync_copy(asked_ref.at[pl.ds(0, slabs)], asked_smem.at[pl.ds(0, slabs)])
+
+    along_ring(1, 0)
+    place_plane(0)
+    lax.fori_loop(0, slabs, serve_first, 0)
+    along_ring(2, 0)
+    place_plane(1)
+    lax.fori_loop(0, slabs, serve_second, 0)
+    place_plane(2)
+    lax.fori_loop(0, slabs, serve_third, 0)
+    wait_for(inbox, recv_m)
+
+    wait_for(inbox.at[pl.ds(0, slabs - 1)], send_m)
+
+    @pl.when(at_edge)
+    def _():
+        wait_for(inbox.at[pl.ds(0, slabs)], edge_m)
 
     wait_for(asked_ref.at[pl.ds(0, slabs - 1 + 2 * REACH)], send_q)
 
@@ -324,23 +425,26 @@
     rows, share = side // slabs, slabs // groups
     ids = np.arange(side)
     angle = 2.0 * np.pi / side * (ids[:, None] * ids[None, :] % side)
-    tables = split_table(np.cos(angle)) + split_table(np.sin(angle))
+    tables = jnp.stack(split_table(np.cos(angle)) + split_table(np.sin(angle)))
     count = groups * slabs
     twist = 2.0 * np.pi / count * (bit_reversed(groups)[:, None] * np.arange(slabs)[None, :])
     scale = 1.0 / math.sqrt(side * side * count)
     twiddle = np.stack([np.cos(twist), np.sin(twist)], axis=-1) * scale
     twiddle = jnp.asarray(twiddle.reshape(-1).astype(np.float32))
-    vmem = pl.BlockSpec(memory_space=pltpu.VMEM)
+    vmem, hbm = pl.BlockSpec(memory_space=pltpu.VMEM), pl.BlockSpec(memory_space=pltpu.HBM)
     f32 = jnp.float32
     return pl.pallas_call(
         functools.partial(transform_kernel, groups, slabs),
-        out_shape=(
-            jax.ShapeDtypeStruct((components, side // LANES, side + 8, LANES), f32),
-            jax.ShapeDtypeStruct((2 * slabs, 1, LANES), jnp.int32),
-        ),
-        in_specs=[vmem] * 6 + [pl.BlockSpec(memory_space=pltpu.SMEM)],
-        out_specs=(vmem, vmem),
+        out_shape=jax.ShapeDtypeStruct((slabs + 2 * REACH, ROWS_OUT, LANES), f32),
+        in_specs=[vmem, hbm, hbm, pl.BlockSpec(memory_space=pltpu.SMEM)],
+        out_specs=vmem,
         scratch_shapes=[
+            pltpu.VMEM((2, components, side, side), f32),
+            pltpu.VMEM((4, side, side), jnp.bfloat16),
+            pltpu.VMEM((2 * slabs, 1, LANES), jnp.int32),
+            pltpu.SMEM((2 * slabs, 1, LANES), jnp.int32),
+            pltpu.VMEM((components, 2, side // 8 + 1, 8, LANES), f32),
+            pltpu.VMEM((slabs, ROWS_OUT, LANES), f32),
             pltpu.VMEM((components, 2, side, side), f32),
             pltpu.VMEM((components, slabs, 2, rows, side), f32),
             pltpu.VMEM((components, slabs, 2, rows, side), f32),
@@ -349,127 +453,26 @@
             pltpu.VMEM((components, side, side), f32),
         ]
         + [pltpu.SemaphoreType.DMA((components,))] * 6
-        + [pltpu.SemaphoreType.DMA] * 2,
+        + [pltpu.SemaphoreType.DMA] * 2
+        + [pltpu.SemaphoreType.DMA((components,))]
+        + [pltpu.SemaphoreType.DMA] * 4,
         compiler_params=pltpu.CompilerParams(
-            collective_id=0, has_side_effects=True, vmem_limit_bytes=40 * 2**20
+            collective_id=0, has_side_effects=True, vmem_limit_bytes=62 * 2**20
         ),
         cost_estimate=pl.CostEstimate(flops=2_500_000_000, bytes_accessed=100_000_000, transcendentals=0),
-    )(asking, spectrum[:, :, 0], *tables, twiddle)
-
-
-def cut_kernel(plane_ref, request_ref, message_ref):
-    slabs = message_ref.shape[0]
-    s = lax.axis_index("gz")
-    lane = lax.broadcasted_iota(jnp.int32, (16, LANES), 1)
-    low_half = lax.broadcasted_iota(jnp.int32, (8, LANES), 0) < 4
-
-    def serve(home, carry):
-        cut = [jnp.zeros((16, LANES), jnp.float32) for _ in range(3)]
-        for slot in range(2 * PLANES):
-            centre = s + slot // 2 - REACH
-            inside = jnp.logical_and(centre >= 0, centre < slabs)
-            row = jnp.where(inside, home, home + slabs)
-            column = 4 * lax.rem(centre + slabs, slabs) + 2 * (slot % 2)
-            start = pl.multiple_of(request_ref[row, 0, column], 8)
-            first = request_ref[row, 0, column + 1]
-            half = first >> 7
-            first = first & (LANES - 1)
-            taken = jnp.logical_and(lane >= CELLS * slot, lane < CELLS * (slot + 1))
-            near = lane >= first
-            for c in range(3):
-                cells = jnp.where(
-                    near,
-                    plane_ref[c, half, pl.ds(start, 16), :],
-                    plane_ref[c, 1 - half, pl.ds(start, 16), :],
-                )
-                moved = pltpu.roll(cells, (CELLS * slot + LANES - first) & (LANES - 1), 1)
-                cut[c] = jnp.where(taken, moved, cut[c])
-        for c in range(3):
-            message_ref[home, 8 * c : 8 * c + 8, :] = cut[c][0:8]
-        message_ref[home, 24:32, :] = jnp.where(low_half, cut[0][8:16], pltpu.roll(cut[1][8:16], 4, 0))
-        message_ref[home, 32:40, :] = cut[2][8:16]
-        return carry
-
-    lax.fori_loop(0, slabs, serve, 0)
-
-
-def exchange_kernel(groups, slabs, message, inbox, send_sem, edge_sem, recv_sem):
-    g = lax.axis_index("grp")
-    s = lax.axis_index("gz")
-    below, above = lax.rem(g + groups - 1, groups), lax.rem(g + 1, groups)
-    at_start, at_end = s < REACH, s >= slabs - REACH
-    at_edge = jnp.logical_or(at_start, at_end)
-
-    barrier = pltpu.get_barrier_semaphore()
-
-    def greet_slab(i, carry):
-        pl.semaphore_signal(barrier, inc=1, device_id=(g, lax.rem(s + i, slabs)), device_id_type=MESH)
-        return carry
-
-    lax.fori_loop(1, slabs, greet_slab, 0)
-    for k in range(REACH):
-        pl.semaphore_signal(barrier, inc=1, device_id=(below, slabs - 1 - k), device_id_type=MESH)
-        pl.semaphore_signal(barrier, inc=1, device_id=(above, k), device_id_type=MESH)
-
-    @pl.when(at_edge)
-    def _():
-        pl.semaphore_wait(barrier, 2 * slabs - 1)
-
-    @pl.when(jnp.logical_not(at_edge))
-    def _():
-        pl.semaphore_wait(barrier, slabs - 1)
-
-    edge_group = jnp.where(at_start, below, above)
-    edge_place = jnp.where(at_start, slabs + REACH + s, s - (slabs - REACH))
-
-    def send(i, carry):
-        home = nearby(s, i, slabs)
-
-        @pl.when(at_edge)
-        def _():
-            pltpu.make_async_remote_copy(
-                src_ref=message.at[home],
-                dst_ref=inbox.at[edge_place],
-                send_sem=edge_sem,
-                recv_sem=recv_sem,
-                device_id=(edge_group, home),
-                device_id_type=MESH,
-            ).start()
-
-        @pl.when(i == 0)
-        def _():
-            pltpu.make_async_copy(message.at[home], inbox.at[REACH + s], recv_sem).start()
-
-        @pl.when(i > 0)
-        def _():
-            pltpu.make_async_remote_copy(
-                src_ref=message.at[home],
-                dst_ref=inbox.at[REACH + s],
-                send_sem=send_sem,
-                recv_sem=recv_sem,
-                device_id=(g, home),
-                device_id_type=MESH,
-            ).start()
-
-        return carry
-
-    lax.fori_loop(0, slabs, send, 0)
-    wait_for(inbox, recv_sem)
-    wait_for(inbox.at[pl.ds(0, slabs - 1)], send_sem)
-
-    @pl.when(at_edge)
-    def _():
-        wait_for(inbox.at[pl.ds(0, slabs)], edge_sem)
+    )(asking, spectrum[:, :, 0], tables, twiddle)
 
 
 def interpolate_kernel(inbox, home_ref, fraction_ref, offset_ref, out_ref, weights):
     blocks, markers = fraction_ref.shape[1], fraction_ref.shape[2]
     weights[...] = jnp.zeros_like(weights)
+    group = weights.shape[0]
+    first_lanes = lax.broadcasted_iota(jnp.int32, (ROWS_OUT * PLANES, LANES), 1) < 16
     row_y = lax.broadcasted_iota(jnp.int32, (16, markers), 0)
     row_x = jnp.where(row_y < 12, row_y, row_y - 4)
     in_low = lax.broadcasted_iota(jnp.int32, (8, markers), 0) < 4
 
-    def interpolate(i, carry):
+    def one_block(i, weights):
         f = jnp.concatenate([fraction_ref[d, pl.ds(i, 1), :] for d in range(3)], axis=0)
         o = [offset_ref[d, pl.ds(i, 1), :] for d in range(3)]
         root = jnp.sqrt(1.0 + 4.0 * f - 4.0 * f * f)
@@ -481,8 +484,9 @@
             weight_x = jnp.where(row_x == o[1] + e, taps[e][1:2], weight_x)
             weight_y = jnp.where(row_y == o[2] + e, taps[e][2:3], weight_y)
         y_high, y_low = split(weight_y)
-        weights[0, 0:16, :] = y_high
-        weights[1, 0:16, :] = y_low
+        weights[0:16, :] = y_high
+        weights[16:32, :] = y_low
+        weights[LANES : LANES + 16, :] = y_high
         near = o[0] == 0
         none = jnp.zeros((1, markers), jnp.float32)
         tap_z = [none] + [tap[0:1] for tap in taps] + [none]
@@ -493,8 +497,9 @@
         for j in range(PLANES):
             place = CELLS * (2 * (PLANES - 1 - j) + slot)
             cells.append(pltpu.roll(inbox[source + j], (2 * LANES - place) & (LANES - 1), 1))
-        cells_high, cells_low = split(jnp.concatenate(cells, axis=0))
-        values = dot(cells_high, weights[0]) + (dot(cells_low, weights[0]) + dot(cells_high, weights[1]))
+        cells = jnp.concatenate(cells, axis=0)
+        cells = jnp.where(first_lanes, cells, pltpu.roll(cells, 16, 1))
+        values = dot(jnp.concatenate(split(cells), axis=1), weights[...])
         sums = []
         for t in range(ROWS_OUT // 8):
             total = weight_z[0] * values[8 * t : 8 * t + 8]
@@ -502,40 +507,28 @@
                 total = total + weight_z[j] * values[ROWS_OUT * j + 8 * t : ROWS_OUT * j + 8 * t + 8]
             sums.append(total)
         x_first, x_last = weight_x[0:8], weight_x[8:16]
-        mixed, last = sums[3] * x_last, sums[4] * x_last
+        mixed, last = sums[2] * x_last, sums[4] * x_last
         tails = (jnp.where(in_low, mixed, 0.0), jnp.where(in_low, 0.0, mixed), jnp.where(in_low, last, 0.0))
         for c in range(3):
-            out_ref[c, pl.ds(i, 1), :] = jnp.sum(sums[c] * x_first + tails[c], axis=0, keepdims=True)
-        return carry
-
-    lax.fori_loop(0, blocks, interpolate, 0)
-
-
-def sample(plane, requests, home, fraction, offsets, groups, slabs):
+            out_ref[c, pl.ds(i, 1), :] = jnp.sum(sums[(0, 1, 3)[c]] * x_first + tails[c], axis=0, keepdims=True)
+
+    def several(i, carry):
+        for k in range(group):
+            one_block(group * i + k, weights.at[k])
+        return carry
+
+    lax.fori_loop(0, blocks // group, several, 0)
+
+
+def sample(inbox, home, fraction, offsets):
     vmem, smem = pl.BlockSpec(memory_space=pltpu.VMEM), pl.BlockSpec(memory_space=pltpu.SMEM)
     markers = fraction.shape[2]
-    message = pl.pallas_call(
-        cut_kernel,
-        out_shape=jax.ShapeDtypeStruct((slabs, ROWS_OUT, LANES), jnp.float32),
-        in_specs=[vmem, smem],
-        out_specs=vmem,
-        cost_estimate=pl.CostEstimate(flops=5_000_000, bytes_accessed=1_500_000, transcendentals=0),
-    )(plane, requests)
-    inbox = pl.pallas_call(
-        functools.partial(exchange_kernel, groups, slabs),
-        out_shape=jax.ShapeDtypeStruct((slabs + 2 * REACH, ROWS_OUT, LANES), jnp.float32),
-        in_specs=[vmem],
-        out_specs=vmem,
-        scratch_shapes=[pltpu.SemaphoreType.DMA] * 3,
-        compiler_params=pltpu.CompilerParams(collective_id=1, has_side_effects=True),
-        cost_estimate=pl.CostEstimate(flops=0, bytes_accessed=20_000_000, transcendentals=0),
-    )(message)
     return pl.pallas_call(
         interpolate_kernel,
         out_shape=jax.ShapeDtypeStruct(fraction.shape, jnp.float32),
         in_specs=[vmem, smem, vmem, vmem],
         out_specs=vmem,
-        scratch_shapes=[pltpu.VMEM((2, LANES, markers), jnp.bfloat16)],
+        scratch_shapes=[pltpu.VMEM((4, 2 * LANES, markers), jnp.bfloat16)],
         cost_estimate=pl.CostEstimate(flops=200_000_000, bytes_accessed=1_500_000, transcendentals=25_000),
     )(inbox, home, fraction, offsets)
 
@@ -548,7 +541,7 @@
     first = jnp.min(jnp.where(named, code[None, :], side * side * blocks), axis=1)
     second = jnp.max(jnp.where(named, code[None, :], 0), axis=1)
     chosen = jnp.stack([first, second], axis=1)
-    starts = jnp.stack([8 * (chosen // side % side), (8 * (chosen % side) - 2 + side) % side], axis=2)
+    starts = jnp.stack([chosen // side % side, (8 * (chosen % side) - 2 + side) % side], axis=2)
     return jnp.pad(starts.reshape(1, -1), ((0, 0), (0, LANES - 4 * slabs)))
 
 
@@ -558,9 +551,10 @@
     order = jnp.arange(source.shape[0])
     again = jnp.any((source[:, None] == source[None, :]) & (order[:, None] > order[None, :]), axis=1)
     home = jnp.concatenate([source, again.astype(jnp.int32)])
-    plane, asked = synthesize(asking, spectrum, groups, slabs)
+    asking, home = lax.optimization_barrier((asking, home))
+    inbox = synthesize(asking, spectrum, groups, slabs)
     fraction, offsets = jnp.transpose(marker_fraction, (1, 0, 2)), jnp.transpose(marker_offsets, (1, 0, 2))
-    answer = sample(plane, asked, home, fraction, offsets, groups, slabs)
+    answer = sample(inbox, home, fraction, offsets)
     return jnp.transpose(answer, (1, 0, 2))
 
 

time: 129 us -> 105 us (0.81); the launches traced: 127 us -> 105 us
  Pallas kernels: 117 us -> 100 us
  local copies, waits for them, and re-layouts: 7.45 us -> 0.76 us
  other arithmetic: 2.33 us -> 3.74 us
    pallas_call x2 -> x0, Pallas kernels: 34.6 us -> none  [the longest x1 27.2 us: sample(): pl.pallas_call(functools.partial(exchange_kernel, groups, slabs), out_sha...]
    pallas_call x1, Pallas kernels: 70.6 us -> 94.7 us  [synthesize(): pl.pallas_call(functools.partial(transform_kernel, groups, slabs), out_sh...]
    unnamed x18 -> x0, local copies, waits for them, and re-layouts: 7.2 us -> none
    pallas_call x1, Pallas kernels: 11.7 us -> 5.74 us  [sample(): pl.pallas_call(interpolate_kernel, out_shape=jax.ShapeDtypeStruct(fractio...]
where the time goes in v2:
time: 105 us
  Pallas kernels  100 us (95%)
  other arithmetic  3.74 us (4%)
    pallas_call x1, Pallas kernels, synthesize(): pl.pallas_call(functools.partial(transform_kernel, groups, slabs), out_sh...  94.7 us
    pallas_call x1, Pallas kernels, sample(): pl.pallas_call(interpolate_kernel, out_shape=jax.ShapeDtypeStruct(fractio...  5.74 us

profile of v2, /device:TPU:1, one launch (start us, length us, event | category | flops | bytes accessed | tf_op | source)
XLA Modules:
  0.0 105.0 jit_solution(4240168765194935987)
XLA Ops:
  0.0 0.9 fusion.1
  0.9 1.3 %pad_add_fusion.2.home_ref = s32[64]{0:T(128)} fusion(s32[32]{0:T(128)S(1)} %convert_element_type.3, s32[32]{0:T(128)} %bitcast.20), kind=kLoop, calls=%fused_computation.23 | loop fusion | flops 64 | bytes 512 | tf_op jit(solution)/shard_map/concatenate | solution.py:553
  2.2 0.8 bitcast_add_fusion
  2.9 0.8 select_reduce_fusion.1
  3.8 0.1 copy.13
  3.9 0.7 reshape.307.asking_ref
  4.5 94.7 %shard_map.100.inbox = f32[36,40,128]{2,1,0:T(8,128)} custom-call(s32[1,128]{1,0:T(1,128)} %reshape.307.asking_ref, f32[2,3,256,256]{3,2,1,0:T(8,128)} %bitcast.22, bf16[4,256,256]{2,1,0:T(8,128)(2,1)} %constant.78.table_hbm, f32[512]{0:T(512)} %constant.68.clone.twiddle_ref), custom_call_target="tpu_custom_call" | custom-call | flops 2500000000 | bytes 100000000 | tf_op jit(solution)/shard_map/pallas_call | solution.py:436
  99.3 5.7 %shard_map.101 = f32[3,32,256]{2,1,0:T(8,128)} custom-call(f32[36,40,128]{2,1,0:T(8,128)} %shard_map.100.inbox, s32[64]{0:T(128)} %pad_add_fusion.2.home_ref, f32[3,32,256]{2,1,0:T(8,128)} %bitcast.15, s32[3,32,256]{2,1,0:T(8,128)} %bitcast.16), custom_call_target="tpu_custom_call" | custom-call | flops 200000000 | bytes 1500000 | tf_op jit(solution)/shard_map/pallas_call | solution.py:526
  (4 shorter events, 0.1 us)

commit v3 on v2

--- a/solution.py
+++ b/solution.py
@@ -88,11 +88,13 @@
 def transform_kernel(
     groups,
     slabs,
-    asking_ref,
+    source_ref,
+    tile_ref,
     spec_hbm,
     table_hbm,
     twiddle_ref,
     inbox,
+    asking_ref,
     spec_ref,
     table,
     asked_ref,
@@ -186,6 +188,25 @@
         ).start()
         lax.fori_loop(1, slabs, one, 0)
 
+    def make_requests():
+        blocks = source_ref.shape[1]
+        down = lax.broadcasted_iota(jnp.int32, (blocks, blocks), 0)
+        along = lax.broadcasted_iota(jnp.int32, (blocks, blocks), 1)
+        tiles = side // 8
+        code = (along[0:1] * tiles + tile_ref[0:1, :]) * tiles + tile_ref[1:2, :]
+
+        def upright(row):
+            return jnp.sum(jnp.where(down == along, row.astype(jnp.float32), 0.0), axis=1, keepdims=True)
+
+        spot = lax.broadcasted_iota(jnp.int32, (blocks, LANES), 1)
+        named = upright(source_ref[...]) == (spot >> 2).astype(jnp.float32)
+        codes = upright(code)
+        first = jnp.min(jnp.where(named, codes, float(tiles * tiles * blocks)), axis=0, keepdims=True)
+        second = jnp.max(jnp.where(named, codes, 0.0), axis=0, keepdims=True)
+        chosen = jnp.where((spot[0:1] & 2) == 0, first, second).astype(jnp.int32)
+        across = (chosen & (tiles - 1)) * 8 + side - REACH
+        asking_ref[...] = jnp.where((spot[0:1] & 1) == 0, (chosen // tiles) & (tiles - 1), across & (side - 1))
+
     def ask(place, device):
         pltpu.make_async_remote_copy(
             src_ref=asking_ref,
@@ -204,6 +225,7 @@
     transform_plane(0)
     pl.semaphore_wait(barrier, slabs - 1 + groups - 1 + 2 * REACH)
     send_rows(0)
+    make_requests()
     pltpu.make_async_copy(asking_ref, asked_ref.at[s], recv_q).start()
     lax.fori_loop(1, slabs, ask_slab, 0)
     for k in range(REACH):
@@ -212,7 +234,6 @@
 
     def later_plane(c, carry):
         transform_plane(c)
-        send_rows(c)
         return carry
 
     lax.fori_loop(1, components, later_plane, 0)
@@ -220,8 +241,7 @@
     inner = min(8, slabs)
     outer = slabs // inner
 
-    def along_slab(c, carry):
-        wait_for(rows_in.at[c], recv_a.at[c])
+    def along_slab(c):
         for block in range(outer):
             items = {k: (rows_in[c, inner * block + k, 0], rows_in[c, inner * block + k, 1]) for k in range(inner)}
             items = butterflies(items, 1, lambda k: k)
@@ -237,6 +257,7 @@
                 rows_z[c, w, 0] = cosine * re - sine * im
                 rows_z[c, w, 1] = sine * re + cosine * im
 
+    def send_ring(c):
         def one(i, inner_carry):
             to = nearby(g, i, groups)
             pltpu.make_async_remote_copy(
@@ -251,12 +272,8 @@
 
         pltpu.make_async_copy(rows_z.at[c, pl.ds(g * share, share)], ring_in.at[c, g], recv_b.at[c]).start()
         lax.fori_loop(1, groups, one, 0)
-        return carry
-
-    lax.fori_loop(0, components, along_slab, 0)
-
-    def along_ring(c, carry):
-        wait_for(ring_in.at[c], recv_b.at[c])
+
+    def along_ring(c):
         for k in range(share):
             items = {q: (ring_in[c, q, k, 0], ring_in[c, q, k, 1]) for q in range(groups)}
             items = butterflies(items, 1, lambda q: q, real_at_end=True)
@@ -288,7 +305,6 @@
             return inner_carry
 
         lax.fori_loop(0, slabs, one, 0)
-        return carry
 
 
     edge_place = jnp.where(at_start, slabs + REACH + s, s - (slabs - REACH))
@@ -302,13 +318,17 @@
             whole = [velocity[c, side - REACH : side, columns], velocity[c, :, columns], velocity[c, 0 : 8 - REACH, columns]]
             padded[c, half] = jnp.concatenate(whole, axis=0).reshape(side // 8 + 1, 8, LANES)
 
+    spots = []
+    for slot in range(2 * PLANES):
+        centre = s + slot // 2 - REACH
+        inside = jnp.logical_and(centre >= 0, centre < slabs)
+        column = 4 * lax.rem(centre + slabs, slabs) + 2 * (slot % 2)
+        spots.append((jnp.where(inside, 0, slabs), column))
+
     def cut_for(c, home):
         cut = jnp.zeros((16, LANES), jnp.float32)
         for slot in range(2 * PLANES):
-            centre = s + slot // 2 - REACH
-            inside = jnp.logical_and(centre >= 0, centre < slabs)
-            row = jnp.where(inside, home, home + slabs)
-            column = 4 * lax.rem(centre + slabs, slabs) + 2 * (slot % 2)
+            row, column = home + spots[slot][0], spots[slot][1]
             tile = asked_smem[row, 0, column]
             first = asked_smem[row, 0, column + 1]
             half = first >> 7
@@ -371,7 +391,14 @@
         deliver(home, i, (3, 4))
         return carry
 
-    along_ring(0, 0)
+    wait_for(rows_in.at[0], recv_a.at[0])
+    send_rows(1)
+    along_slab(0)
+    send_ring(0)
+    wait_for(rows_in.at[1], recv_a.at[1])
+    send_rows(2)
+    along_slab(1)
+    send_ring(1)
 
     @pl.when(at_edge)
     def _():
@@ -383,10 +410,17 @@
         wait_for(asked_ref.at[pl.ds(0, slabs)], recv_q)
         pltpu.sync_copy(asked_ref.at[pl.ds(0, slabs)], asked_smem.at[pl.ds(0, slabs)])
 
-    along_ring(1, 0)
+    wait_for(ring_in.at[0], recv_b.at[0])
+    along_ring(0)
+    wait_for(rows_in.at[2], recv_a.at[2])
+    along_slab(2)
+    wait_for(ring_in.at[1], recv_b.at[1])
+    send_ring(2)
+    along_ring(1)
     place_plane(0)
     lax.fori_loop(0, slabs, serve_first, 0)
-    along_ring(2, 0)
+    wait_for(ring_in.at[2], recv_b.at[2])
+    along_ring(2)
     place_plane(1)
     lax.fori_loop(0, slabs, serve_second, 0)
     place_plane(2)
@@ -420,7 +454,7 @@
     lax.fori_loop(0, components, drain, 0)
 
 
-def synthesize(asking, spectrum, groups, slabs):
+def synthesize(source, tiles, spectrum, groups, slabs):
     components, side = spectrum.shape[1], spectrum.shape[3]
     rows, share = side // slabs, slabs // groups
     ids = np.arange(side)
@@ -436,9 +470,10 @@
     return pl.pallas_call(
         functools.partial(transform_kernel, groups, slabs),
         out_shape=jax.ShapeDtypeStruct((slabs + 2 * REACH, ROWS_OUT, LANES), f32),
-        in_specs=[vmem, hbm, hbm, pl.BlockSpec(memory_space=pltpu.SMEM)],
+        in_specs=[vmem, vmem, hbm, hbm, pl.BlockSpec(memory_space=pltpu.SMEM)],
         out_specs=vmem,
         scratch_shapes=[
+            pltpu.VMEM((1, LANES), jnp.int32),
             pltpu.VMEM((2, components, side, side), f32),
             pltpu.VMEM((4, side, side), jnp.bfloat16),
             pltpu.VMEM((2 * slabs, 1, LANES), jnp.int32),
@@ -460,10 +495,10 @@
             collective_id=0, has_side_effects=True, vmem_limit_bytes=62 * 2**20
         ),
         cost_estimate=pl.CostEstimate(flops=2_500_000_000, bytes_accessed=100_000_000, transcendentals=0),
-    )(asking, spectrum[:, :, 0], tables, twiddle)
-
-
-def interpolate_kernel(inbox, home_ref, fraction_ref, offset_ref, out_ref, weights):
+    )(source, tiles, spectrum[:, :, 0], tables, twiddle)
+
+
+def interpolate_kernel(inbox, source_ref, fraction_ref, offset_ref, out_ref, weights, named):
     blocks, markers = fraction_ref.shape[1], fraction_ref.shape[2]
     weights[...] = jnp.zeros_like(weights)
     group = weights.shape[0]
@@ -471,6 +506,9 @@
     row_y = lax.broadcasted_iota(jnp.int32, (16, markers), 0)
     row_x = jnp.where(row_y < 12, row_y, row_y - 4)
     in_low = lax.broadcasted_iota(jnp.int32, (8, markers), 0) < 4
+
+    for k in range(named.shape[0]):
+        named[k] = 0
 
     def one_block(i, weights):
         f = jnp.concatenate([fraction_ref[d, pl.ds(i, 1), :] for d in range(3)], axis=0)
@@ -491,8 +529,9 @@
         none = jnp.zeros((1, markers), jnp.float32)
         tap_z = [none] + [tap[0:1] for tap in taps] + [none]
         weight_z = [jnp.where(near, tap_z[j + 1], tap_z[j]) for j in range(PLANES)]
-        source = home_ref[i]
-        slot = home_ref[blocks + i]
+        source = source_ref[0, i]
+        slot = named[source]
+        named[source] = 1
         cells = []
         for j in range(PLANES):
             place = CELLS * (2 * (PLANES - 1 - j) + slot)
@@ -520,7 +559,7 @@
     lax.fori_loop(0, blocks // group, several, 0)
 
 
-def sample(inbox, home, fraction, offsets):
+def sample(inbox, source, fraction, offsets, slabs):
     vmem, smem = pl.BlockSpec(memory_space=pltpu.VMEM), pl.BlockSpec(memory_space=pltpu.SMEM)
     markers = fraction.shape[2]
     return pl.pallas_call(
@@ -528,33 +567,16 @@
         out_shape=jax.ShapeDtypeStruct(fraction.shape, jnp.float32),
         in_specs=[vmem, smem, vmem, vmem],
         out_specs=vmem,
-        scratch_shapes=[pltpu.VMEM((4, 2 * LANES, markers), jnp.bfloat16)],
+        scratch_shapes=[pltpu.VMEM((4, 2 * LANES, markers), jnp.bfloat16), pltpu.SMEM((slabs,), jnp.int32)],
         cost_estimate=pl.CostEstimate(flops=200_000_000, bytes_accessed=1_500_000, transcendentals=25_000),
-    )(inbox, home, fraction, offsets)
-
-
-def patch_requests(source, block_tile, slabs, side):
-    blocks = source.shape[0]
-    order = jnp.arange(blocks, dtype=jnp.int32)
-    code = (order * side + block_tile[:, 0]) * side + block_tile[:, 1]
-    named = source[None, :] == jnp.arange(slabs, dtype=jnp.int32)[:, None]
-    first = jnp.min(jnp.where(named, code[None, :], side * side * blocks), axis=1)
-    second = jnp.max(jnp.where(named, code[None, :], 0), axis=1)
-    chosen = jnp.stack([first, second], axis=1)
-    starts = jnp.stack([chosen // side % side, (8 * (chosen % side) - 2 + side) % side], axis=2)
-    return jnp.pad(starts.reshape(1, -1), ((0, 0), (0, LANES - 4 * slabs)))
+    )(inbox, source, fraction, offsets)
 
 
 def local(groups, slabs, spectrum, marker_fraction, marker_offsets, block_source, block_tile):
-    source = block_source[:, 0]
-    asking = patch_requests(source, block_tile, slabs, spectrum.shape[3])
-    order = jnp.arange(source.shape[0])
-    again = jnp.any((source[:, None] == source[None, :]) & (order[:, None] > order[None, :]), axis=1)
-    home = jnp.concatenate([source, again.astype(jnp.int32)])
-    asking, home = lax.optimization_barrier((asking, home))
-    inbox = synthesize(asking, spectrum, groups, slabs)
+    source = jnp.transpose(block_source)
+    inbox = synthesize(source, jnp.transpose(block_tile), spectrum, groups, slabs)
     fraction, offsets = jnp.transpose(marker_fraction, (1, 0, 2)), jnp.transpose(marker_offsets, (1, 0, 2))
-    answer = sample(inbox, home, fraction, offsets)
+    answer = sample(inbox, source, fraction, offsets, slabs)
     return jnp.transpose(answer, (1, 0, 2))
 
 

time: 105 us -> 95 us (0.905); the launches traced: 105 us -> 93.7 us
  Pallas kernels: 100 us -> 93.7 us
  other arithmetic: 3.74 us -> 0 us
    pallas_call x1, Pallas kernels: 94.7 us -> 87.9 us  [synthesize(): pl.pallas_call(functools.partial(transform_kernel, groups, slabs), out_sh...]
    concatenate x1 -> x0, other arithmetic: 1.25 us -> none  [local(): home = jnp.concatenate([source, again.astype(jnp.int32)])]
where the time goes in v3:
time: 95 us; the launch traced here: 93.7 us
  Pallas kernels  93.7 us (99%)
    pallas_call x1, Pallas kernels, synthesize(): pl.pallas_call(functools.partial(transform_kernel, groups, slabs), out_sh...  87.9 us
    pallas_call x1, Pallas kernels, sample(): pl.pallas_call(interpolate_kernel, out_shape=jax.ShapeDtypeStruct(fractio...  5.78 us

profile of v3, /device:TPU:1, one launch (start us, length us, event | category | flops | bytes accessed | tf_op | source)
XLA Modules:
  0.0 93.7 jit_solution(1911150411810875751)
XLA Ops:
  0.0 87.9 %shard_map.100.inbox = f32[36,40,128]{2,1,0:T(8,128)} custom-call(s32[1,32]{1,0:T(1,128)} %bitcast.8, s32[2,32]{1,0:T(2,128)} %bitcast.11, f32[2,3,256,256]{3,2,1,0:T(8,128)} %bitcast.10, bf16[4,256,256]{2,1,0:T(8,128)(2,1)} %constant.24.table_hbm, f32[512]{0:T(512)} %constant.14.clone.twiddle_ref), custom_call_target="tpu_custom_call" | custom-call | flops 2500000000 | bytes 100000000 | tf_op jit(solution)/shard_map/pallas_call | solution.py:470
  87.9 5.8 %shard_map.101 = f32[3,32,256]{2,1,0:T(8,128)} custom-call(f32[36,40,128]{2,1,0:T(8,128)} %shard_map.100.inbox, s32[1,32]{1,0:T(1,128)} %bitcast.9, f32[3,32,256]{2,1,0:T(8,128)} %bitcast.6, s32[3,32,256]{2,1,0:T(8,128)} %bitcast.7), custom_call_target="tpu_custom_call" | custom-call | flops 200000000 | bytes 1500000 | tf_op jit(solution)/shard_map/pallas_call | solution.py:565

commit v4 on v3

--- a/solution.py
+++ b/solution.py
@@ -165,8 +165,12 @@
         re, im = split(spec_ref[0, c]), split(spec_ref[1, c])
         row_re = split(dot3(re, cosine) - dot3(im, sine))
         row_im = split(dot3(re, sine) + dot3(im, cosine))
-        plane_t[c, 0] = dot3(cosine, row_re) - dot3(sine, row_im)
-        plane_t[c, 1] = dot3(sine, row_re) + dot3(cosine, row_im)
+        for part, whole in (
+            (0, dot3(cosine, row_re) - dot3(sine, row_im)),
+            (1, dot3(sine, row_re) + dot3(cosine, row_im)),
+        ):
+            for half in range(2):
+                plane_t[2 * c + half, part] = whole[:, half * LANES : (half + 1) * LANES]
 
     def send_rows(c):
         def one(i, carry):
@@ -232,11 +236,9 @@
         ask(slabs + s, (below, slabs - 1 - k))
         ask(slabs + s, (above, k))
 
-    def later_plane(c, carry):
-        transform_plane(c)
-        return carry
-
-    lax.fori_loop(1, components, later_plane, 0)
+    transform_plane(1)
+    send_rows(1)
+    transform_plane(2)
 
     inner = min(8, slabs)
     outer = slabs // inner
@@ -312,10 +314,10 @@
     lane = lax.broadcasted_iota(jnp.int32, (16, LANES), 1)
 
     def place_plane(c):
-        wait_for(velocity.at[c], recv_c.at[c])
         for half in range(2):
-            columns = slice(half * LANES, (half + 1) * LANES)
-            whole = [velocity[c, side - REACH : side, columns], velocity[c, :, columns], velocity[c, 0 : 8 - REACH, columns]]
+            got = velocity.at[2 * c + half]
+            wait_for(got, recv_c.at[2 * c + half])
+            whole = [got[side - REACH : side, :], got[...], got[0 : 8 - REACH, :]]
             padded[c, half] = jnp.concatenate(whole, axis=0).reshape(side // 8 + 1, 8, LANES)
 
     spots = []
@@ -391,13 +393,23 @@
         deliver(home, i, (3, 4))
         return carry
 
-    wait_for(rows_in.at[0], recv_a.at[0])
-    send_rows(1)
-    along_slab(0)
+    parts = 2 * components
+
+    def spread(k):
+        wait_for(rows_in.at[k], recv_a.at[k])
+        if k + 2 < parts:
+            send_rows(k + 2)
+        along_slab(k)
+
+    def gather(k):
+        wait_for(ring_in.at[k], recv_b.at[k])
+        if k + 2 < parts:
+            send_ring(k + 2)
+        along_ring(k)
+
+    spread(0)
     send_ring(0)
-    wait_for(rows_in.at[1], recv_a.at[1])
-    send_rows(2)
-    along_slab(1)
+    spread(1)
     send_ring(1)
 
     @pl.when(at_edge)
@@ -410,17 +422,13 @@
         wait_for(asked_ref.at[pl.ds(0, slabs)], recv_q)
         pltpu.sync_copy(asked_ref.at[pl.ds(0, slabs)], asked_smem.at[pl.ds(0, slabs)])
 
-    wait_for(ring_in.at[0], recv_b.at[0])
-    along_ring(0)
-    wait_for(rows_in.at[2], recv_a.at[2])
-    along_slab(2)
-    wait_for(ring_in.at[1], recv_b.at[1])
-    send_ring(2)
-    along_ring(1)
+    for k in range(2, parts):
+        spread(k)
+        gather(k - 2)
     place_plane(0)
     lax.fori_loop(0, slabs, serve_first, 0)
-    wait_for(ring_in.at[2], recv_b.at[2])
-    along_ring(2)
+    gather(parts - 2)
+    gather(parts - 1)
     place_plane(1)
     lax.fori_loop(0, slabs, serve_second, 0)
     place_plane(2)
@@ -451,12 +459,12 @@
 
         return carry
 
-    lax.fori_loop(0, components, drain, 0)
+    lax.fori_loop(0, 2 * components, drain, 0)
 
 
 def synthesize(source, tiles, spectrum, groups, slabs):
     components, side = spectrum.shape[1], spectrum.shape[3]
-    rows, share = side // slabs, slabs // groups
+    rows, share, parts = side // slabs, slabs // groups, components * side // LANES
     ids = np.arange(side)
     angle = 2.0 * np.pi / side * (ids[:, None] * ids[None, :] % side)
     tables = jnp.stack(split_table(np.cos(angle)) + split_table(np.sin(angle)))
@@ -480,14 +488,14 @@
             pltpu.SMEM((2 * slabs, 1, LANES), jnp.int32),
             pltpu.VMEM((components, 2, side // 8 + 1, 8, LANES), f32),
             pltpu.VMEM((slabs, ROWS_OUT, LANES), f32),
-            pltpu.VMEM((components, 2, side, side), f32),
-            pltpu.VMEM((components, slabs, 2, rows, side), f32),
-            pltpu.VMEM((components, slabs, 2, rows, side), f32),
-            pltpu.VMEM((components, groups, share, 2, rows, side), f32),
-            pltpu.VMEM((components, groups, share, rows, side), f32),
-            pltpu.VMEM((components, side, side), f32),
+            pltpu.VMEM((parts, 2, side, LANES), f32),
+            pltpu.VMEM((parts, slabs, 2, rows, LANES), f32),
+            pltpu.VMEM((parts, slabs, 2, rows, LANES), f32),
+            pltpu.VMEM((parts, groups, share, 2, rows, LANES), f32),
+            pltpu.VMEM((parts, groups, share, rows, LANES), f32),
+            pltpu.VMEM((parts, side, LANES), f32),
         ]
-        + [pltpu.SemaphoreType.DMA((components,))] * 6
+        + [pltpu.SemaphoreType.DMA((parts,))] * 6
         + [pltpu.SemaphoreType.DMA] * 2
         + [pltpu.SemaphoreType.DMA((components,))]
         + [pltpu.SemaphoreType.DMA] * 4,

time: 95 us -> 93.1 us (0.980)
  Pallas kernels: 93.7 us -> 91.6 us
    pallas_call x1, Pallas kernels: 87.9 us -> 85.8 us  [synthesize(): pl.pallas_call(functools.partial(transform_kernel, groups, slabs), out_sh...]
where the time goes in v4:
time: 93.1 us; the launch traced here: 91.6 us
  Pallas kernels  91.6 us (98%)
    pallas_call x1, Pallas kernels, synthesize(): pl.pallas_call(functools.partial(transform_kernel, groups, slabs), out_sh...  85.8 us
    pallas_call x1, Pallas kernels, sample(): pl.pallas_call(interpolate_kernel, out_shape=jax.ShapeDtypeStruct(fractio...  5.77 us

profile of v4, /device:TPU:1, one launch (start us, length us, event | category | flops | bytes accessed | tf_op | source)
XLA Modules:
  0.0 91.6 jit_solution(6613772057220465869)
XLA Ops:
  0.0 85.8 %shard_map.100.inbox = f32[36,40,128]{2,1,0:T(8,128)} custom-call(s32[1,32]{1,0:T(1,128)} %bitcast.8, s32[2,32]{1,0:T(2,128)} %bitcast.11, f32[2,3,256,256]{3,2,1,0:T(8,128)} %bitcast.10, bf16[4,256,256]{2,1,0:T(8,128)(2,1)} %constant.24.table_hbm, f32[512]{0:T(512)} %constant.14.clone.twiddle_ref), custom_call_target="tpu_custom_call" | custom-call | flops 2500000000 | bytes 100000000 | tf_op jit(solution)/shard_map/pallas_call | solution.py:478
  85.8 5.8 %shard_map.101 = f32[3,32,256]{2,1,0:T(8,128)} custom-call(f32[36,40,128]{2,1,0:T(8,128)} %shard_map.100.inbox, s32[1,32]{1,0:T(1,128)} %bitcast.9, f32[3,32,256]{2,1,0:T(8,128)} %bitcast.6, s32[3,32,256]{2,1,0:T(8,128)} %bitcast.7), custom_call_target="tpu_custom_call" | custom-call | flops 200000000 | bytes 1500000 | tf_op jit(solution)/shard_map/pallas_call | solution.py:573

commit v5 on v4

--- a/solution.py
+++ b/solution.py
@@ -229,16 +229,8 @@
     transform_plane(0)
     pl.semaphore_wait(barrier, slabs - 1 + groups - 1 + 2 * REACH)
     send_rows(0)
-    make_requests()
-    pltpu.make_async_copy(asking_ref, asked_ref.at[s], recv_q).start()
-    lax.fori_loop(1, slabs, ask_slab, 0)
-    for k in range(REACH):
-        ask(slabs + s, (below, slabs - 1 - k))
-        ask(slabs + s, (above, k))
-
     transform_plane(1)
     send_rows(1)
-    transform_plane(2)
 
     inner = min(8, slabs)
     outer = slabs // inner
@@ -343,7 +335,7 @@
             cut = jnp.where(taken, moved, cut)
         return cut
 
-    def deliver(home, i, tiles):
+    def deliver(home, own, tiles):
         part = pl.ds(8 * tiles[0], 8 * len(tiles))
 
         @pl.when(at_edge)
@@ -357,12 +349,10 @@
                 device_id_type=MESH,
             ).start()
 
-        @pl.when(i == 0)
-        def _():
+        def keep():
             pltpu.make_async_copy(message.at[home, part], inbox.at[REACH + s, part], recv_m).start()
 
-        @pl.when(i > 0)
-        def _():
+        def give():
             pltpu.make_async_remote_copy(
                 src_ref=message.at[home, part],
                 dst_ref=inbox.at[REACH + s, part],
@@ -372,25 +362,39 @@
                 device_id_type=MESH,
             ).start()
 
+        if own is None:
+            give()
+        else:
+            pl.when(own)(keep)
+            pl.when(jnp.logical_not(own))(give)
+
+    at_once = 4
+
+    def homes_of(i):
+        return [nearby(s, at_once * i + k, slabs) for k in range(at_once)]
+
     def serve_first(i, carry):
-        home = nearby(s, i, slabs)
-        cut = cut_for(0, home)
-        message[home, 0:8, :] = cut[0:8]
-        message[home, 16:24, :] = cut[8:16]
+        homes = homes_of(i)
+        for home, cut in zip(homes, [cut_for(0, home) for home in homes]):
+            message[home, 0:8, :] = cut[0:8]
+            message[home, 16:24, :] = cut[8:16]
         return carry
 
     def serve_second(i, carry):
-        home = nearby(s, i, slabs)
-        cut = cut_for(1, home)
-        message[home, 8:16, :] = cut[0:8]
-        message[home, 16:24, :] = jnp.where(low_half, message[home, 16:24, :], pltpu.roll(cut[8:16], 4, 0))
-        deliver(home, i, (0, 1, 2))
+        homes = homes_of(i)
+        for home, cut in zip(homes, [cut_for(1, home) for home in homes]):
+            message[home, 8:16, :] = cut[0:8]
+            message[home, 16:24, :] = jnp.where(low_half, message[home, 16:24, :], pltpu.roll(cut[8:16], 4, 0))
+        for k, home in enumerate(homes):
+            deliver(home, None if k else i == 0, (0, 1, 2))
         return carry
 
     def serve_third(i, carry):
-        home = nearby(s, i, slabs)
-        message[home, 24:40, :] = cut_for(2, home)
-        deliver(home, i, (3, 4))
+        homes = homes_of(i)
+        for home, cut in zip(homes, [cut_for(2, home) for home in homes]):
+            message[home, 24:40, :] = cut
+        for k, home in enumerate(homes):
+            deliver(home, None if k else i == 0, (3, 4))
         return carry
 
     parts = 2 * components
@@ -409,9 +413,19 @@
 
     spread(0)
     send_ring(0)
+    make_requests()
+    pltpu.make_async_copy(asking_ref, asked_ref.at[s], recv_q).start()
+    lax.fori_loop(1, slabs, ask_slab, 0)
+    for k in range(REACH):
+        ask(slabs + s, (below, slabs - 1 - k))
+        ask(slabs + s, (above, k))
+    transform_plane(2)
     spread(1)
     send_ring(1)
 
+    for k in range(2, parts):
+        spread(k)
+        gather(k - 2)
     @pl.when(at_edge)
     def _():
         wait_for(asked_ref, recv_q)
@@ -422,17 +436,14 @@
         wait_for(asked_ref.at[pl.ds(0, slabs)], recv_q)
         pltpu.sync_copy(asked_ref.at[pl.ds(0, slabs)], asked_smem.at[pl.ds(0, slabs)])
 
-    for k in range(2, parts):
-        spread(k)
-        gather(k - 2)
     place_plane(0)
-    lax.fori_loop(0, slabs, serve_first, 0)
+    lax.fori_loop(0, slabs // at_once, serve_first, 0)
     gather(parts - 2)
     gather(parts - 1)
     place_plane(1)
-    lax.fori_loop(0, slabs, serve_second, 0)
+    lax.fori_loop(0, slabs // at_once, serve_second, 0)
     place_plane(2)
-    lax.fori_loop(0, slabs, serve_third, 0)
+    lax.fori_loop(0, slabs // at_once, serve_third, 0)
     wait_for(inbox, recv_m)
 
     wait_for(inbox.at[pl.ds(0, slabs - 1)], send_m)
@@ -575,7 +586,7 @@
         out_shape=jax.ShapeDtypeStruct(fraction.shape, jnp.float32),
         in_specs=[vmem, smem, vmem, vmem],
         out_specs=vmem,
-        scratch_shapes=[pltpu.VMEM((4, 2 * LANES, markers), jnp.bfloat16), pltpu.SMEM((slabs,), jnp.int32)],
+        scratch_shapes=[pltpu.VMEM((8, 2 * LANES, markers), jnp.bfloat16), pltpu.SMEM((slabs,), jnp.int32)],
         cost_estimate=pl.CostEstimate(flops=200_000_000, bytes_accessed=1_500_000, transcendentals=25_000),
     )(inbox, source, fraction, offsets)
 

time: 93.1 us -> 92.1 us (0.989)
  Pallas kernels: 91.6 us -> 90.5 us
    pallas_call x1, Pallas kernels: 5.77 us -> 4.8 us  [sample(): pl.pallas_call(interpolate_kernel, out_shape=jax.ShapeDtypeStruct(fractio...]
where the time goes in v5:
time: 92.1 us; the launch traced here: 90.5 us
  Pallas kernels  90.5 us (98%)
    pallas_call x1, Pallas kernels, synthesize(): pl.pallas_call(functools.partial(transform_kernel, groups, slabs), out_sh...  85.7 us
    pallas_call x1, Pallas kernels, sample(): pl.pallas_call(interpolate_kernel, out_shape=jax.ShapeDtypeStruct(fractio...  4.8 us

profile of v5, /device:TPU:1, one launch (start us, length us, event | category | flops | bytes accessed | tf_op | source)
XLA Modules:
  0.0 90.5 jit_solution(13004874271543111767)
XLA Ops:
  0.0 85.7 %shard_map.100.inbox = f32[36,40,128]{2,1,0:T(8,128)} custom-call(s32[1,32]{1,0:T(1,128)} %bitcast.8, s32[2,32]{1,0:T(2,128)} %bitcast.11, f32[2,3,256,256]{3,2,1,0:T(8,128)} %bitcast.10, bf16[4,256,256]{2,1,0:T(8,128)(2,1)} %constant.24.table_hbm, f32[512]{0:T(512)} %constant.14.clone.twiddle_ref), custom_call_target="tpu_custom_call" | custom-call | flops 2500000000 | bytes 100000000 | tf_op jit(solution)/shard_map/pallas_call | solution.py:489
  85.7 4.8 %shard_map.101 = f32[3,32,256]{2,1,0:T(8,128)} custom-call(f32[36,40,128]{2,1,0:T(8,128)} %shard_map.100.inbox, s32[1,32]{1,0:T(1,128)} %bitcast.9, f32[3,32,256]{2,1,0:T(8,128)} %bitcast.6, s32[3,32,256]{2,1,0:T(8,128)} %bitcast.7), custom_call_target="tpu_custom_call" | custom-call | flops 200000000 | bytes 1500000 | tf_op jit(solution)/shard_map/pallas_call | solution.py:584

commit v6 on v5

--- a/solution.py
+++ b/solution.py
@@ -404,24 +404,21 @@
         if k + 2 < parts:
             send_rows(k + 2)
         along_slab(k)
+        send_ring(k)
 
     def gather(k):
         wait_for(ring_in.at[k], recv_b.at[k])
-        if k + 2 < parts:
-            send_ring(k + 2)
         along_ring(k)
 
     spread(0)
-    send_ring(0)
+    spread(1)
+    transform_plane(2)
     make_requests()
     pltpu.make_async_copy(asking_ref, asked_ref.at[s], recv_q).start()
     lax.fori_loop(1, slabs, ask_slab, 0)
     for k in range(REACH):
         ask(slabs + s, (below, slabs - 1 - k))
         ask(slabs + s, (above, k))
-    transform_plane(2)
-    spread(1)
-    send_ring(1)
 
     for k in range(2, parts):
         spread(k)

time: 92.1 us -> 92.1 us (level)
  no operation moved by 1% of the time
where the time goes in v6:
time: 92.1 us; the launch traced here: 90.5 us
  Pallas kernels  90.5 us (98%)
    pallas_call x1, Pallas kernels, synthesize(): pl.pallas_call(functools.partial(transform_kernel, groups, slabs), out_sh...  85.7 us
    pallas_call x1, Pallas kernels, sample(): pl.pallas_call(interpolate_kernel, out_shape=jax.ShapeDtypeStruct(fractio...  4.79 us

profile of v6, /device:TPU:1, one launch (start us, length us, event | category | flops | bytes accessed | tf_op | source)
XLA Modules:
  0.0 90.5 jit_solution(8470623650070123814)
XLA Ops:
  0.0 85.7 %shard_map.100.inbox = f32[36,40,128]{2,1,0:T(8,128)} custom-call(s32[1,32]{1,0:T(1,128)} %bitcast.8, s32[2,32]{1,0:T(2,128)} %bitcast.11, f32[2,3,256,256]{3,2,1,0:T(8,128)} %bitcast.10, bf16[4,256,256]{2,1,0:T(8,128)(2,1)} %constant.24.table_hbm, f32[512]{0:T(512)} %constant.14.clone.twiddle_ref), custom_call_target="tpu_custom_call" | custom-call | flops 2500000000 | bytes 100000000 | tf_op jit(solution)/shard_map/pallas_call | solution.py:486
  85.7 4.8 %shard_map.101 = f32[3,32,256]{2,1,0:T(8,128)} custom-call(f32[36,40,128]{2,1,0:T(8,128)} %shard_map.100.inbox, s32[1,32]{1,0:T(1,128)} %bitcast.9, f32[3,32,256]{2,1,0:T(8,128)} %bitcast.6, s32[3,32,256]{2,1,0:T(8,128)} %bitcast.7), custom_call_target="tpu_custom_call" | custom-call | flops 200000000 | bytes 1500000 | tf_op jit(solution)/shard_map/pallas_call | solution.py:581

commit v7 on v6

--- a/solution.py
+++ b/solution.py
@@ -120,6 +120,8 @@
     send_m,
     edge_m,
     recv_m,
+    send_e,
+    recv_e,
 ):
     g = lax.axis_index("grp")
     s = lax.axis_index("gz")
@@ -143,21 +145,12 @@
         pl.semaphore_signal(barrier, inc=1, device_id=(g, lax.rem(s + i, slabs)), device_id_type=MESH)
         return carry
 
-    def greet_edge(i, carry):
-        pl.semaphore_signal(barrier, inc=1, device_id=(edge_group, lax.rem(s + i, slabs)), device_id_type=MESH)
-        return carry
-
     def greet_ring(i, carry):
         pl.semaphore_signal(barrier, inc=1, device_id=(lax.rem(g + i, groups), s), device_id_type=MESH)
         return carry
 
     lax.fori_loop(1, slabs, greet_slab, 0)
     lax.fori_loop(1, groups, greet_ring, 0)
-
-    @pl.when(at_edge)
-    def _():
-        lax.fori_loop(0, slabs, greet_edge, 0)
-
 
     def transform_plane(c):
         pltpu.make_async_copy(spec_hbm.at[:, c], spec_ref.at[:, c], load_sem.at[c]).wait()
@@ -227,7 +220,7 @@
 
     loads[0].wait()
     transform_plane(0)
-    pl.semaphore_wait(barrier, slabs - 1 + groups - 1 + 2 * REACH)
+    pl.semaphore_wait(barrier, slabs - 1 + groups - 1)
     send_rows(0)
     transform_plane(1)
     send_rows(1)
@@ -416,22 +409,25 @@
     make_requests()
     pltpu.make_async_copy(asking_ref, asked_ref.at[s], recv_q).start()
     lax.fori_loop(1, slabs, ask_slab, 0)
-    for k in range(REACH):
-        ask(slabs + s, (below, slabs - 1 - k))
-        ask(slabs + s, (above, k))
-
     for k in range(2, parts):
         spread(k)
         gather(k - 2)
+    wait_for(asked_ref.at[pl.ds(0, slabs)], recv_q)
+    pltpu.sync_copy(asked_ref.at[pl.ds(0, slabs)], asked_smem.at[pl.ds(0, slabs)])
+
     @pl.when(at_edge)
     def _():
-        wait_for(asked_ref, recv_q)
-        pltpu.sync_copy(asked_ref, asked_smem)
-
-    @pl.when(jnp.logical_not(at_edge))
-    def _():
-        wait_for(asked_ref.at[pl.ds(0, slabs)], recv_q)
-        pltpu.sync_copy(asked_ref.at[pl.ds(0, slabs)], asked_smem.at[pl.ds(0, slabs)])
+        passed = pltpu.make_async_remote_copy(
+            src_ref=asked_ref.at[pl.ds(0, slabs)],
+            dst_ref=asked_ref.at[pl.ds(slabs, slabs)],
+            send_sem=send_e,
+            recv_sem=recv_e,
+            device_id=(jnp.where(at_start, above, below), s),
+            device_id_type=MESH,
+        )
+        passed.start()
+        passed.wait()
+        pltpu.sync_copy(asked_ref.at[pl.ds(slabs, slabs)], asked_smem.at[pl.ds(slabs, slabs)])
 
     place_plane(0)
     lax.fori_loop(0, slabs // at_once, serve_first, 0)
@@ -449,7 +445,7 @@
     def _():
         wait_for(inbox.at[pl.ds(0, slabs)], edge_m)
 
-    wait_for(asked_ref.at[pl.ds(0, slabs - 1 + 2 * REACH)], send_q)
+    wait_for(asked_ref.at[pl.ds(0, slabs - 1)], send_q)
 
     holds_own = lax.div(s, share) == g
 
@@ -506,7 +502,7 @@
         + [pltpu.SemaphoreType.DMA((parts,))] * 6
         + [pltpu.SemaphoreType.DMA] * 2
         + [pltpu.SemaphoreType.DMA((components,))]
-        + [pltpu.SemaphoreType.DMA] * 4,
+        + [pltpu.SemaphoreType.DMA] * 6,
         compiler_params=pltpu.CompilerParams(
             collective_id=0, has_side_effects=True, vmem_limit_bytes=62 * 2**20
         ),

time: 92.1 us -> 95.4 us (1.036)
  Pallas kernels: 90.5 us -> 94.6 us
    pallas_call x1, Pallas kernels: 85.7 us -> 89.8 us  [synthesize(): pl.pallas_call(functools.partial(transform_kernel, groups, slabs), out_sh...]
where the time goes in v7:
time: 95.4 us; the launch traced here: 94.6 us
  Pallas kernels  94.6 us (99%)
    pallas_call x1, Pallas kernels, synthesize(): pl.pallas_call(functools.partial(transform_kernel, groups, slabs), out_sh...  89.8 us
    pallas_call x1, Pallas kernels, sample(): pl.pallas_call(interpolate_kernel, out_shape=jax.ShapeDtypeStruct(fractio...  4.8 us

profile of v7, /device:TPU:1, one launch (start us, length us, event | category | flops | bytes accessed | tf_op | source)
XLA Modules:
  0.0 94.6 jit_solution(8694455232258510267)
XLA Ops:
  0.0 89.8 %shard_map.100.inbox = f32[36,40,128]{2,1,0:T(8,128)} custom-call(s32[1,32]{1,0:T(1,128)} %bitcast.8, s32[2,32]{1,0:T(2,128)} %bitcast.11, f32[2,3,256,256]{3,2,1,0:T(8,128)} %bitcast.10, bf16[4,256,256]{2,1,0:T(8,128)(2,1)} %constant.24.table_hbm, f32[512]{0:T(512)} %constant.14.clone.twiddle_ref), custom_call_target="tpu_custom_call" | custom-call | flops 2500000000 | bytes 100000000 | tf_op jit(solution)/shard_map/pallas_call | solution.py:482
  89.8 4.8 %shard_map.101 = f32[3,32,256]{2,1,0:T(8,128)} custom-call(f32[36,40,128]{2,1,0:T(8,128)} %shard_map.100.inbox, s32[1,32]{1,0:T(1,128)} %bitcast.9, f32[3,32,256]{2,1,0:T(8,128)} %bitcast.6, s32[3,32,256]{2,1,0:T(8,128)} %bitcast.7), custom_call_target="tpu_custom_call" | custom-call | flops 200000000 | bytes 1500000 | tf_op jit(solution)/shard_map/pallas_call | solution.py:577

commit v8 on v7

--- a/solution.py
+++ b/solution.py
@@ -409,25 +409,33 @@
     make_requests()
     pltpu.make_async_copy(asking_ref, asked_ref.at[s], recv_q).start()
     lax.fori_loop(1, slabs, ask_slab, 0)
-    for k in range(2, parts):
-        spread(k)
-        gather(k - 2)
-    wait_for(asked_ref.at[pl.ds(0, slabs)], recv_q)
-    pltpu.sync_copy(asked_ref.at[pl.ds(0, slabs)], asked_smem.at[pl.ds(0, slabs)])
+    spread(2)
+    gather(0)
+
+    own_asked, more_asked = pl.ds(0, slabs), pl.ds(slabs, slabs)
+    wait_for(asked_ref.at[own_asked], recv_q)
 
     @pl.when(at_edge)
     def _():
-        passed = pltpu.make_async_remote_copy(
-            src_ref=asked_ref.at[pl.ds(0, slabs)],
-            dst_ref=asked_ref.at[pl.ds(slabs, slabs)],
+        pltpu.make_async_remote_copy(
+            src_ref=asked_ref.at[own_asked],
+            dst_ref=asked_ref.at[more_asked],
             send_sem=send_e,
             recv_sem=recv_e,
             device_id=(jnp.where(at_start, above, below), s),
             device_id_type=MESH,
-        )
-        passed.start()
-        passed.wait()
-        pltpu.sync_copy(asked_ref.at[pl.ds(slabs, slabs)], asked_smem.at[pl.ds(slabs, slabs)])
+        ).start()
+
+    pltpu.sync_copy(asked_ref.at[own_asked], asked_smem.at[own_asked])
+    for k in range(3, parts):
+        spread(k)
+        gather(k - 2)
+
+    @pl.when(at_edge)
+    def _():
+        wait_for(asked_ref.at[more_asked], recv_e)
+        wait_for(asked_ref.at[own_asked], send_e)
+        pltpu.sync_copy(asked_ref.at[more_asked], asked_smem.at[more_asked])
 
     place_plane(0)
     lax.fori_loop(0, slabs // at_once, serve_first, 0)

time: 95.4 us -> 91 us (0.954)
  Pallas kernels: 94.6 us -> 89.7 us
    pallas_call x1, Pallas kernels: 89.8 us -> 84.9 us  [synthesize(): pl.pallas_call(functools.partial(transform_kernel, groups, slabs), out_sh...]
where the time goes in v8:
time: 91 us; the launch traced here: 89.7 us
  Pallas kernels  89.7 us (99%)
    pallas_call x1, Pallas kernels, synthesize(): pl.pallas_call(functools.partial(transform_kernel, groups, slabs), out_sh...  84.9 us
    pallas_call x1, Pallas kernels, sample(): pl.pallas_call(interpolate_kernel, out_shape=jax.ShapeDtypeStruct(fractio...  4.8 us

profile of v8, /device:TPU:1, one launch (start us, length us, event | category | flops | bytes accessed | tf_op | source)
XLA Modules:
  0.0 89.7 jit_solution(9242737113633140973)
XLA Ops:
  0.0 84.9 %shard_map.100.inbox = f32[36,40,128]{2,1,0:T(8,128)} custom-call(s32[1,32]{1,0:T(1,128)} %bitcast.8, s32[2,32]{1,0:T(2,128)} %bitcast.11, f32[2,3,256,256]{3,2,1,0:T(8,128)} %bitcast.10, bf16[4,256,256]{2,1,0:T(8,128)(2,1)} %constant.24.table_hbm, f32[512]{0:T(512)} %constant.14.clone.twiddle_ref), custom_call_target="tpu_custom_call" | custom-call | flops 2500000000 | bytes 100000000 | tf_op jit(solution)/shard_map/pallas_call | solution.py:490
  84.9 4.8 %shard_map.101 = f32[3,32,256]{2,1,0:T(8,128)} custom-call(f32[36,40,128]{2,1,0:T(8,128)} %shard_map.100.inbox, s32[1,32]{1,0:T(1,128)} %bitcast.9, f32[3,32,256]{2,1,0:T(8,128)} %bitcast.6, s32[3,32,256]{2,1,0:T(8,128)} %bitcast.7), custom_call_target="tpu_custom_call" | custom-call | flops 200000000 | bytes 1500000 | tf_op jit(solution)/shard_map/pallas_call | solution.py:585

commit v9 on v8

--- a/solution.py
+++ b/solution.py
@@ -244,12 +244,17 @@
                 rows_z[c, w, 0] = cosine * re - sine * im
                 rows_z[c, w, 1] = sine * re + cosine * im
 
-    def send_ring(c):
+    real_only = g < 2
+
+    def send_ring_parts(c, count):
+        def piece(to):
+            return rows_z.at[c, pl.ds(to * share, share), pl.ds(0, count)]
+
         def one(i, inner_carry):
             to = nearby(g, i, groups)
             pltpu.make_async_remote_copy(
-                src_ref=rows_z.at[c, pl.ds(to * share, share)],
-                dst_ref=ring_in.at[c, g],
+                src_ref=piece(to),
+                dst_ref=ring_in.at[c, g, :, pl.ds(0, count)],
                 send_sem=send_b.at[c],
                 recv_sem=recv_b.at[c],
                 device_id=(to, s),
@@ -257,12 +262,21 @@
             ).start()
             return inner_carry
 
-        pltpu.make_async_copy(rows_z.at[c, pl.ds(g * share, share)], ring_in.at[c, g], recv_b.at[c]).start()
+        pltpu.make_async_copy(piece(g), ring_in.at[c, g, :, pl.ds(0, count)], recv_b.at[c]).start()
         lax.fori_loop(1, groups, one, 0)
+
+    def send_ring(c):
+        @pl.when(real_only)
+        def _():
+            send_ring_parts(c, 1)
+
+        @pl.when(jnp.logical_not(real_only))
+        def _():
+            send_ring_parts(c, 2)
 
     def along_ring(c):
         for k in range(share):
-            items = {q: (ring_in[c, q, k, 0], ring_in[c, q, k, 1]) for q in range(groups)}
+            items = {q: (ring_in[c, q, k, 0], ring_in[c, q, k, 1] if q > 1 else jnp.zeros((rows, LANES), jnp.float32)) for q in range(groups)}
             items = butterflies(items, 1, lambda q: q, real_at_end=True)
             for u in range(groups):
                 real_z[c, u, k] = items[u][0]
@@ -400,7 +414,7 @@
         send_ring(k)
 
     def gather(k):
-        wait_for(ring_in.at[k], recv_b.at[k])
+        wait_for(ring_in.at[k, pl.ds(0, groups - 1)], recv_b.at[k])
         along_ring(k)
 
     spread(0)
@@ -459,7 +473,13 @@
 
     def drain(c, carry):
         wait_for(rows_in.at[c, pl.ds(0, slabs - 1)], send_a.at[c])
-        wait_for(ring_in.at[c, pl.ds(0, groups - 1)], send_b.at[c])
+        @pl.when(real_only)
+        def _():
+            wait_for(ring_in.at[c, pl.ds(0, groups - 1), :, pl.ds(0, 1)], send_b.at[c])
+
+        @pl.when(jnp.logical_not(real_only))
+        def _():
+            wait_for(ring_in.at[c, pl.ds(0, groups - 1)], send_b.at[c])
 
         @pl.when(holds_own)
         def _():

time: 91 us -> 91.3 us (level)
  no operation moved by 1% of the time
where the time goes in v9:
time: 91.3 us; the launch traced here: 89.6 us
  Pallas kernels  89.6 us (98%)
    pallas_call x1, Pallas kernels, synthesize(): pl.pallas_call(functools.partial(transform_kernel, groups, slabs), out_sh...  84.8 us
    pallas_call x1, Pallas kernels, sample(): pl.pallas_call(interpolate_kernel, out_shape=jax.ShapeDtypeStruct(fractio...  4.8 us

profile of v9, /device:TPU:1, one launch (start us, length us, event | category | flops | bytes accessed | tf_op | source)
XLA Modules:
  0.0 89.6 jit_solution(12901875829743440505)
XLA Ops:
  0.0 84.8 %shard_map.100.inbox = f32[36,40,128]{2,1,0:T(8,128)} custom-call(s32[1,32]{1,0:T(1,128)} %bitcast.8, s32[2,32]{1,0:T(2,128)} %bitcast.11, f32[2,3,256,256]{3,2,1,0:T(8,128)} %bitcast.10, bf16[4,256,256]{2,1,0:T(8,128)(2,1)} %constant.24.table_hbm, f32[512]{0:T(512)} %constant.14.clone.twiddle_ref), custom_call_target="tpu_custom_call" | custom-call | flops 2500000000 | bytes 100000000 | tf_op jit(solution)/shard_map/pallas_call | solution.py:510
  84.8 4.8 %shard_map.101 = f32[3,32,256]{2,1,0:T(8,128)} custom-call(f32[36,40,128]{2,1,0:T(8,128)} %shard_map.100.inbox, s32[1,32]{1,0:T(1,128)} %bitcast.9, f32[3,32,256]{2,1,0:T(8,128)} %bitcast.6, s32[3,32,256]{2,1,0:T(8,128)} %bitcast.7), custom_call_target="tpu_custom_call" | custom-call | flops 200000000 | bytes 1500000 | tf_op jit(solution)/shard_map/pallas_call | solution.py:605
